TPU v7x, 256 devices: a whole 4x4x8 slice. The times are simulated.
256 devices in a mesh: dp: 16 (over x, y), context: 16 (over z, core).
Axes of the slice: x: 4, y: 4, z: 8, core: 2. Of those that a mesh axis runs over, the one named last changes fastest.
Arguments:
- queries: bfloat16 [65536, 512], P(('dp', 'context')), may hold values from -6 to 6
- keys: bfloat16 [65536, 128], P(('dp', 'context')), may hold values from -6 to 6
- values: bfloat16 [65536, 128], P(('dp', 'context')), may hold values from -6 to 6
- doc_ids: int32 [65536], P(('dp', 'context')), may hold values from 0 to 63, never falling along the last dimension, each value on 1 to 2048 neighbouring positions
Outputs:
- attended: bfloat16 [65536, 512], P(('dp', 'context'))
Inputs may be any that keep to these rules, and one draw needn't show every extreme that they name: `doc_ids`: Non-decreasing along the tokens; no document has more than 2048 tokens, and one has exactly 2048.
All inputs are finite; a program needn't handle non-finite values.
Results may differ from a plain program's by a relative error of at most 0.0037.
Values may be sent and summed in bfloat16 or wider, within the bound.
No kernel may reach another device: no remote copies, remote signals or barrier semaphores. Data moves between devices by JAX's collectives and lax.ppermute only.
A program may use at most 128 MiB of HBM per device.

v0:
```python
import math

import jax
import jax.numpy as jnp
from jax import lax
from jax.sharding import PartitionSpec as P

masked_score = -1e30


def shifted(value, axis, steps):
    count = lax.axis_size(axis)
    first, last = (max(0, -steps), min(count, count - steps))
    return lax.ppermute(value, axis, [(source, source + steps) for source in range(first, last)])


def attend(carry, query_rows, query_pos, query_ids, piece, first, scale):
    key_block, value_block, key_docs = piece
    key_pos = first + jnp.arange(key_block.shape[0], dtype=jnp.int32)
    allowed = (
        (query_ids[:, None] == key_docs[None, :])
        & (key_pos[None, :] <= query_pos[:, None])
        & (key_pos[None, :] >= 0)
    )
    top, total, weighted = carry
    scores = (
        jnp.einsum("qhd,kd->hqk", query_rows, key_block, preferred_element_type=jnp.float32) * scale
    )
    scores = jnp.where(allowed[None], scores, masked_score)
    new_top = jnp.maximum(top, jnp.max(scores, axis=-1))
    raised = jnp.where(allowed[None], jnp.exp(scores - new_top[..., None]), 0.0)
    fade = jnp.exp(top - new_top)
    total = total * fade + jnp.sum(raised, axis=-1)
    weighted = weighted * fade[..., None] + jnp.einsum(
        "hqk,kd->hqd", raised.astype(jnp.bfloat16), value_block, preferred_element_type=jnp.float32
    )
    return (new_top, total, weighted)


def body(queries, keys, values, doc_ids):
    rows = queries.shape[0]
    width = keys.shape[1]
    heads = queries.shape[1] // width
    n_context = lax.axis_size("context")
    device = lax.axis_index("dp") * n_context + lax.axis_index("context")
    group_base = lax.axis_index("dp") * n_context * rows
    query_ids = doc_ids.astype(jnp.bfloat16)
    scale = 1.0 / math.sqrt(width)
    query_rows = queries.reshape(rows, heads, width)
    query_pos = device * rows + jnp.arange(rows, dtype=jnp.int32)
    state = (
        jnp.full((heads, rows), masked_score, jnp.float32),
        jnp.zeros((heads, rows), jnp.float32),
        jnp.zeros((heads, rows, width), jnp.float32),
    )

    def absorb(carry, piece, first):
        return attend(carry, query_rows, query_pos, query_ids, piece, first, scale)

    state = absorb(
        state,
        (
            lax.all_gather(keys, "context", axis=0, tiled=True),
            lax.all_gather(values, "context", axis=0, tiled=True),
            lax.all_gather(query_ids, "context", axis=0, tiled=True),
        ),
        group_base,
    )
    prior = shifted((keys, values, query_ids), "dp", 1)
    state = absorb(
        state,
        (
            lax.all_gather(prior[0], "context", axis=0, tiled=True),
            lax.all_gather(prior[1], "context", axis=0, tiled=True),
            lax.all_gather(prior[2], "context", axis=0, tiled=True),
        ),
        group_base - n_context * rows,
    )
    top, total, weighted = state
    result = weighted / total[..., None]
    return jnp.transpose(result, (1, 0, 2)).reshape(rows, heads * width).astype(jnp.bfloat16)


def solution(mesh):
    return jax.shard_map(
        body,
        mesh=mesh,
        in_specs=(
            P(("dp", "context"), None),
            P(("dp", "context"), None),
            P(("dp", "context"), None),
            P(("dp", "context")),
        ),
        out_specs=P(("dp", "context"), None),
        check_vma=False,
    )
```

profile of v0, /device:TPU:35, one launch (start us, length us, event | category | flops | bytes accessed | tf_op | source)
XLA Modules:
  0.0 183.8 jit_solution(7817817379022067580)
XLA Ops:
  6.5 0.7 all-gather.7.cloned.1.call-update
  7.3 0.0 all-gather.11.cloned.1.call-start
  7.3 3.2 %collective-permute-start.1 = (bf16[256,128]{1,0:T(8,128)(2,1)}, bf16[256,128]{1,0:T(8,128)(2,1)S(1)}, u32[]{:S(2)}, u32[]{:S(2)}) collective-permute-start(bf16[256,128]{1,0:T(8,128)(2,1)} %param.5), channel_id=1, source_target_pairs={{0,16},{16,32},{32,48},{48,64},{64,80},{80,96},{96,112},{112,128},... | collective-permute-start | bytes 196616 | tf_op jit(solution)/shard_map/ppermute | solution.py:14
  10.5 4.1 %collective-permute-done.1 = bf16[256,128]{1,0:T(8,128)(2,1)S(1)} collective-permute-done((bf16[256,128]{1,0:T(8,128)(2,1)}, bf16[256,128]{1,0:T(8,128)(2,1)S(1)}, u32[]{:S(2)}, u32[]{:S(2)}) %collective-permute-start.1) | collective-permute-done | bytes 65568 | tf_op jit(solution)/shard_map/ppermute | solution.py:14
  14.6 0.6 copy-done.3
  15.3 0.0 all-gather.9.cloned.1.call-start
  15.3 1.6 copy.20
  16.9 0.0 all-gather.13.cloned.1.call-start
  17.0 1.9 %collective-permute-start.2 = (bf16[256,128]{0,1:T(8,128)(2,1)}, bf16[256,128]{0,1:T(8,128)(2,1)S(1)}, u32[]{:S(2)}, u32[]{:S(2)}) collective-permute-start(bf16[256,128]{0,1:T(8,128)(2,1)} %copy.20), channel_id=1, source_target_pairs={{0,16},{16,32},{32,48},{48,64},{64,80},{80,96},{96,112},{112,128},... | collective-permute-start | bytes 196616 | tf_op jit(solution)/shard_map/ppermute | solution.py:14
  18.9 0.7 convert_element_type.15
  19.6 2.4 %collective-permute-start = (bf16[256]{0:T(256)(128)(2,1)S(1)}, bf16[256]{0:T(256)(128)(2,1)S(1)}, u32[]{:S(2)}, u32[]{:S(2)}) collective-permute-start(bf16[256]{0:T(256)(128)(2,1)S(1)} %convert_element_type.15), channel_id=1, source_target_pairs={{0,16},{16,32},{32,48},{48,64},{64,80},{80,96},{96,112},{112,128},... | collective-permute-start | bytes 1544 | tf_op jit(solution)/shard_map/ppermute | solution.py:14
  22.1 20.1 %all-gather = bf16[16,1,256]{2,1,0:T(2,128)(2,1)S(1)} all-gather(bf16[1,1,256]{2,1,0:T(2,128)(2,1)S(1)} %reshape.194), channel_id=1, replica_groups=mesh['dp'=16,'context'=16] {'context'}, dimensions={0}, use_global_device_ids=true | all-gather | bytes 8704 | tf_op jit(solution)/shard_map/all_gather | solution.py:65
  42.2 16.4 %all-gather.1 = bf16[16,1,256]{2,1,0:T(2,128)(2,1)S(1)} all-gather(bf16[1,1,256]{2,1,0:T(2,128)(2,1)S(1)} %reshape.196), channel_id=1, replica_groups=mesh['dp'=16,'context'=16] {'context'}, dimensions={0}, use_global_device_ids=true | all-gather | bytes 8704 | tf_op jit(solution)/shard_map/all_gather | solution.py:75
  58.6 4.7 %and_and_fusion = (pred[256,4096]{0,1:T(8,128)(4,1)S(1)}, pred[256,4096]{0,1:T(8,128)(4,1)S(1)}) fusion(s32[256]{0:T(256)S(1)} %iota_add_fusion.2, s32[4096]{0:T(1024)S(1)} %iota_add_fusion, pred[4096]{0:T(1024)(128)(4,1)S(1)} %broadcast_compare_fusion, bf16[256]{0:T(256)(128)(2,1)S(1)} %convert_element_type.15, bf16[4096]{0:T(1024)(128)(2,1)S(1)} %bitcast.114, ...), kind=kLoop, calls=%fused_computation.14 | loop fusion | flops 11534336 | bytes 2156032 | tf_op jit(solution)/shard_map/and | solution.py:21
  63.3 0.6 copy-done.2
  64.0 8.5 %fusion = (f32[4,256]{1,0:T(4,128)S(1)}, f32[4096,256,4]{1,0,2:T(8,128)}) fusion(pred[256,4096]{0,1:T(8,128)(4,1)S(1)} %get-tuple-element.11, bf16[4096,128]{1,0:T(8,128)(2,1)} %all-gather.7.cloned.1.call-done, bf16[256,512]{1,0:T(8,128)(2,1)S(1)} %copy-done), kind=kOutput, calls=%fused_computation.4 | convolution fusion | flops 1086323712 | bytes 19140608 | tf_op jit(solution)/shard_map/qhd,kd->hqk/dot_general | solution.py:27
  72.5 16.9 %all-gather.11.cloned.1.call-done = bf16[4096,128]{1,0:T(8,128)(2,1)} async-done(((bf16[256,128]{1,0:T(8,128)(2,1)}), bf16[4096,128]{1,0:T(8,128)(2,1)}) %all-gather.11.cloned.1.call-update) | async-done | bytes 1048592 | tf_op jit(solution)/shard_map/all_gather | solution.py:73
  89.4 3.9 %fusion.1 = (f32[4,256]{1,0:T(4,128)S(1)}, f32[4096,256,4]{1,0,2:T(8,128)S(1)}) fusion(pred[256,4096]{0,1:T(8,128)(4,1)S(1)} %get-tuple-element.10, bf16[4096,128]{1,0:T(8,128)(2,1)} %all-gather.11.cloned.1.call-done, bf16[256,512]{1,0:T(8,128)(2,1)S(1)} %copy-done), kind=kOutput, calls=%fused_computation.5 | convolution fusion | flops 1086323712 | bytes 19140608 | tf_op jit(solution)/shard_map/qhd,kd->hqk/dot_general | solution.py:27
  93.4 16.0 %fusion.2 = (f32[4,256]{1,0:T(4,128)S(1)}, f32[4,256]{1,0:T(4,128)S(1)}) fusion(f32[4096,256,4]{1,0,2:T(8,128)} %get-tuple-element.15, f32[4,256]{1,0:T(4,128)S(1)} %get-tuple-element.9, pred[256,4096]{0,1:T(8,128)(4,1)S(1)} %get-tuple-element.11, f32[4,256]{1,0:T(4,128)S(1)} %get-tuple-element.8, f32[4096,256,4]{1,0,2:T(8,128)S(1)} %get-tuple-element.13, ...), kind=kLoop, calls=%fused_computation.6 | loop fusion | flops 41940992 | bytes 35667968 | tf_op jit(solution)/shard_map/reduce_sum | solution.py:33
  109.4 18.2 %all-gather.9.cloned.1.call-done = bf16[4096,128]{0,1:T(8,128)(2,1)} async-done(((bf16[256,128]{0,1:T(8,128)(2,1)}), bf16[4096,128]{0,1:T(8,128)(2,1)}) %all-gather.9.cloned.1.call-update) | async-done | bytes 1048592 | tf_op jit(solution)/shard_map/all_gather | solution.py:64
  127.6 8.0 %fusion.24 = f32[256,4,128]{0,2,1:T(8,128)S(1)} fusion(f32[4096,256,4]{1,0,2:T(8,128)} %get-tuple-element.15, f32[4,256]{1,0:T(4,128)S(1)} %get-tuple-element.9, pred[256,4096]{0,1:T(8,128)(4,1)S(1)} %get-tuple-element.11, bf16[4096,128]{0,1:T(8,128)(2,1)} %all-gather.9.cloned.1.call-done, f32[256,4]{0,1:T(4,128)S(1)} %get-tuple-element.6, ...), kind=kOutput, calls=%fused_computation.20 | convolution fusion | flops 1094975488 | bytes 19410944 | tf_op jit(solution)/shard_map/hqk,kd->hqd/dot_general | solution.py:34
  135.6 30.4 %all-gather.13.cloned.1.call-done = bf16[4096,128]{0,1:T(8,128)(2,1)} async-done(((bf16[256,128]{0,1:T(8,128)(2,1)}), bf16[4096,128]{0,1:T(8,128)(2,1)}) %all-gather.13.cloned.1.call-update) | async-done | bytes 1048592 | tf_op jit(solution)/shard_map/all_gather | solution.py:74
  166.0 10.4 %fusion.38 = bf16[256,4,128]{0,2,1:T(8,128)(2,1)S(1)} fusion(f32[256,4,128]{0,2,1:T(8,128)S(1)} %fusion.24, f32[4096,256,4]{1,0,2:T(8,128)} %copy-done.1, f32[4,256]{1,0:T(4,128)S(1)} %get-tuple-element.8, pred[256,4096]{0,1:T(8,128)(4,1)S(1)} %get-tuple-element.10, bf16[4096,128]{0,1:T(8,128)(2,1)} %all-gather.13.cloned.1.call-done, ...), kind=kOutput, calls=%fused_computation.28 | convolution fusion | flops 1095106560 | bytes 19668992 | tf_op jit(solution)/shard_map/hqk,kd->hqd/dot_general | solution.py:34
  176.4 0.8 copy.25
  (26 shorter events, 0.3 us)
Async XLA Ops:
  6.5 57.4 %copy-start = (bf16[256,512]{1,0:T(8,128)(2,1)S(1)}, bf16[256,512]{1,0:T(8,128)(2,1)}, u32[]{:S(2)}) copy-start(bf16[256,512]{1,0:T(8,128)(2,1)} %param.4) | copy-start | bytes 786436
  6.5 57.4 %all-gather.7.cloned.1.call-start = ((), (), s32[]{:S(2)}) async-start(), calls=%async_computation | async-start | bytes 1114112 | tf_op jit(solution)/shard_map/all_gather | solution.py:63
  7.3 82.1 %all-gather.11.cloned.1.call-start = ((), (), s32[]{:S(2)}) async-start(), calls=%async_computation.2 | async-start | bytes 1114112 | tf_op jit(solution)/shard_map/all_gather | solution.py:73
  7.3 7.3 %collective-permute-start.1 = (bf16[256,128]{1,0:T(8,128)(2,1)}, bf16[256,128]{1,0:T(8,128)(2,1)S(1)}, u32[]{:S(2)}, u32[]{:S(2)}) collective-permute-start(bf16[256,128]{1,0:T(8,128)(2,1)} %param.5), channel_id=1, source_target_pairs={{0,16},{16,32},{32,48},{48,64},{64,80},{80,96},{96,112},{112,128},... | collective-permute-start | bytes 196616 | tf_op jit(solution)/shard_map/ppermute | solution.py:14
  14.6 0.6 copy-start.3
  15.3 112.3 %all-gather.9.cloned.1.call-start = ((), (), s32[]{:S(2)}) async-start(), calls=%async_computation.1 | async-start | bytes 1114112 | tf_op jit(solution)/shard_map/all_gather | solution.py:64
  16.9 149.1 %all-gather.13.cloned.1.call-start = ((), (), s32[]{:S(2)}) async-start(), calls=%async_computation.3 | async-start | bytes 1114112 | tf_op jit(solution)/shard_map/all_gather | solution.py:74
  17.0 46.3 %collective-permute-start.2 = (bf16[256,128]{0,1:T(8,128)(2,1)}, bf16[256,128]{0,1:T(8,128)(2,1)S(1)}, u32[]{:S(2)}, u32[]{:S(2)}) collective-permute-start(bf16[256,128]{0,1:T(8,128)(2,1)} %copy.20), channel_id=1, source_target_pairs={{0,16},{16,32},{32,48},{48,64},{64,80},{80,96},{96,112},{112,128},... | collective-permute-start | bytes 196616 | tf_op jit(solution)/shard_map/ppermute | solution.py:14
  19.6 22.6 %collective-permute-start = (bf16[256]{0:T(256)(128)(2,1)S(1)}, bf16[256]{0:T(256)(128)(2,1)S(1)}, u32[]{:S(2)}, u32[]{:S(2)}) collective-permute-start(bf16[256]{0:T(256)(128)(2,1)S(1)} %convert_element_type.15), channel_id=1, source_target_pairs={{0,16},{16,32},{32,48},{48,64},{64,80},{80,96},{96,112},{112,128},... | collective-permute-start | bytes 1544 | tf_op jit(solution)/shard_map/ppermute | solution.py:14
  63.3 0.6 copy-start.2
  93.4 16.0 %copy-start.1 = (f32[4096,256,4]{1,0,2:T(8,128)}, f32[4096,256,4]{1,0,2:T(8,128)S(1)}, u32[]{:S(2)}) copy-start(f32[4096,256,4]{1,0,2:T(8,128)S(1)} %get-tuple-element.13) | copy-start | bytes 50331652
Sparse Core Ops, SparseCore 0:
  9.2 40.9 all-gather.6
  52.0 37.3 all-gather.10
  91.2 36.4 all-gather.8
  129.2 36.7 all-gather.12
where the time goes:
time: 186 us; the launch traced here: 184 us
  waiting for transfers between devices  70.5 us (38%)
  blocking collectives  36.4 us (20%)
  matrix products  30.8 us (17%)
  other arithmetic  21.5 us (12%)
  between operations  13.3 us (7%)
  starting transfers between devices  7.61 us (4%)
  local copies, waits for them, and re-layouts  3.68 us (2%)
    all_gather x1, waiting for transfers between devices, body(): lax.all_gather(prior[1], 'context', axis=0, tiled=True)  30.4 us
    all_gather x1, blocking collectives, body(): lax.all_gather(query_ids, 'context', axis=0, tiled=True)  20.1 us
    dot_general x2, matrix products, attend(): jnp.einsum('hqk,kd->hqd', raised.astype(jnp.bfloat16), value_block, prefe...  18.4 us
    all_gather x1, waiting for transfers between devices, body(): lax.all_gather(values, 'context', axis=0, tiled=True)  18.2 us
    all_gather x1, waiting for transfers between devices, body(): lax.all_gather(prior[0], 'context', axis=0, tiled=True)  16.9 us
    all_gather x1, blocking collectives, body(): lax.all_gather(prior[2], 'context', axis=0, tiled=True)  16.4 us
    reduce_sum x1, other arithmetic, attend(): total = total * fade + jnp.sum(raised, axis=-1)  16 us
    dot_general x2, matrix products, attend(): jnp.einsum('qhd,kd->hqk', query_rows, key_block, preferred_element_type=j...  12.4 us
  transfers between devices with their start and end apart: 7, of which 4 were waited for; matrix products, arithmetic and copies ran while one was open for 24% of the time, Pallas kernels for 0%

commit v1 on v0

v1 whole, which is shorter than its diff:
```python
import functools
import math

import jax
import jax.numpy as jnp
from jax import lax
from jax.experimental import pallas as pl
from jax.experimental.pallas import tpu as pltpu
from jax.sharding import PartitionSpec as P

outside = -2e30
lowest = -1e30
axes = ("dp", "context")
pad = 16


def chips_on(value, steps):
    count = lax.axis_size(axes[0]) * lax.axis_size(axes[1])
    shift = 2 * steps
    return lax.ppermute(value, axes, [(d, (d + shift) % count) for d in range(count)])


def both_cores(value):
    count = lax.axis_size("context")
    pairs = [[d, d + 1] for d in range(0, count, 2)]
    return lax.all_gather(value, "context", axis=0, tiled=True, axis_index_groups=pairs)


def core():
    return lax.rem(lax.axis_index("context"), 2)


def nt(a, b):
    return lax.dot_general(a, b, (((1,), (1,)), ((), ())), preferred_element_type=jnp.float32)


def nn(a, b):
    return lax.dot_general(a, b, (((1,), (0,)), ((), ())), preferred_element_type=jnp.float32)


def split(packed, rows, width):
    keys = packed[0:rows, 0:width]
    values = packed[0:rows, width : 2 * width].T
    ids = packed[rows : rows + 1, :].astype(jnp.float32)
    return keys, values, ids


def suffix_mask(ids, wanted, rows):
    matches = jnp.sum(jnp.where(ids == wanted, 1.0, 0.0), axis=1, keepdims=True)
    at = lax.broadcasted_iota(jnp.int32, (rows, rows), 0).astype(jnp.float32)
    return at >= rows - matches


def update(state, pieces, q, scale):
    top, total, acc = state
    scores = [jnp.where(mask, nt(keys, q) * scale, outside) for keys, _, mask in pieces]
    new_top = top
    for s in scores:
        new_top = jnp.maximum(new_top, jnp.max(s, axis=0, keepdims=True))
    fade = jnp.exp2(top - new_top)
    total = total * fade
    acc = acc * fade
    for s, (_, values, _) in zip(scores, pieces):
        raised = jnp.exp2(s - new_top)
        total = total + jnp.sum(raised, axis=0, keepdims=True)
        acc = acc + nn(values, raised.astype(jnp.bfloat16))
    return new_top, total, acc


def sides(q_ref, rows):
    mine = core()
    own = q_ref.at[pl.ds(pl.multiple_of(mine * rows, rows), rows), :]
    twin = q_ref.at[pl.ds(pl.multiple_of((1 - mine) * rows, rows), rows), :]
    return own, twin


def wanted_ids(own_ids, near_ids, rows):
    first = own_ids[:, 0:1]
    last = own_ids[:, rows - 1 : rows]
    near = near_ids[:, rows - 1 : rows]
    return first, jnp.where(core() == 0, last, near)


def early_kernel(scale, heads, q_ref, kv0_ref, kv1_ref, kv4_ref, stat_ref, acc_ref):
    rows, width = kv0_ref.shape[1], kv0_ref.shape[1] // 2
    own_q, twin_q = sides(q_ref, rows)
    keys0, values0, ids0 = split(kv0_ref, rows, width)
    keys1, values1, ids1 = split(kv1_ref, rows, width)
    keys4, values4, ids4 = split(kv4_ref, rows, width)
    first, other = wanted_ids(ids0, ids1, rows)
    at_key = lax.broadcasted_iota(jnp.int32, (rows, rows), 0)
    at_row = lax.broadcasted_iota(jnp.int32, (rows, rows), 1)
    ids_col = jnp.sum(jnp.where(at_key == at_row, ids0, 0.0), axis=1, keepdims=True)
    causal = (ids_col == ids0) & (at_key <= at_row)
    in_first = ids0 == first
    own = [
        (keys0, values0, causal),
        (keys1, values1, suffix_mask(ids1, first, rows) & in_first),
        (keys4, values4, suffix_mask(ids4, first, rows) & in_first),
    ]
    seen = jnp.where(core() == 0, ids0, -1.0)
    twin = [
        (keys0, values0, suffix_mask(seen, other, rows)),
        (keys1, values1, suffix_mask(ids1, other, rows)),
        (keys4, values4, suffix_mask(ids4, other, rows)),
    ]
    for side, (pieces, q) in enumerate(((own, own_q), (twin, twin_q))):
        for head in range(heads):
            state = (
                jnp.full((1, rows), lowest, jnp.float32),
                jnp.zeros((1, rows), jnp.float32),
                jnp.zeros((width, rows), jnp.float32),
            )
            q_head = q[:, head * width : (head + 1) * width]
            top, total, acc = update(state, pieces, q_head, scale)
            at = side * heads + head
            stat_ref[2 * at : 2 * at + 1, :] = top
            stat_ref[2 * at + 1 : 2 * at + 2, :] = total
            acc_ref[at * width : (at + 1) * width, :] = acc


def late_kernel(
    scale, heads, q_ref, kv0_ref, kv1_ref, kv2_ref, kv3_ref, stat_ref, acc_ref, lse_ref, mean_ref, send_ref
):
    rows, width = kv0_ref.shape[1], kv0_ref.shape[1] // 2
    own_q, twin_q = sides(q_ref, rows)
    ids0 = kv0_ref[rows : rows + 1, :].astype(jnp.float32)
    ids1 = kv1_ref[rows : rows + 1, :].astype(jnp.float32)
    keys2, values2, ids2 = split(kv2_ref, rows, width)
    keys3, values3, ids3 = split(kv3_ref, rows, width)
    first, other = wanted_ids(ids0, ids1, rows)
    in_first = ids0 == first
    own = [
        (keys2, values2, suffix_mask(ids2, first, rows) & in_first),
        (keys3, values3, suffix_mask(ids3, first, rows) & in_first),
    ]
    twin = [
        (keys2, values2, suffix_mask(ids2, other, rows)),
        (keys3, values3, suffix_mask(ids3, other, rows)),
    ]
    extra = []
    for side, (pieces, q) in enumerate(((twin, twin_q), (own, own_q))):
        for head in range(heads):
            at = (1 - side) * heads + head
            state = (
                stat_ref[2 * at : 2 * at + 1, :],
                stat_ref[2 * at + 1 : 2 * at + 2, :],
                acc_ref[at * width : (at + 1) * width, :],
            )
            q_head = q[:, head * width : (head + 1) * width]
            top, total, acc = update(state, pieces, q_head, scale)
            some = total > 0.0
            lse = jnp.where(some, top + jnp.log2(jnp.where(some, total, 1.0)), lowest)
            mean = acc * jnp.where(some, 1.0 / jnp.where(some, total, 1.0), 0.0)
            place = slice(head * width, (head + 1) * width)
            if side == 0:
                send_ref[place, :] = mean.astype(jnp.bfloat16)
                rest = lse
                for _ in range(3):
                    part = rest.astype(jnp.bfloat16)
                    extra.append(part.astype(jnp.float32))
                    rest = rest - part.astype(jnp.float32)
            else:
                lse_ref[head : head + 1, :] = lse
                mean_ref[place, :] = mean
    extra.append(jnp.broadcast_to(other, (1, rows)))
    extra.append(jnp.zeros((pad - len(extra), rows), jnp.float32))
    send_ref[heads * width :, :] = jnp.concatenate(extra, axis=0).astype(jnp.bfloat16)


def merge_kernel(heads, kv0_ref, lse_ref, mean_ref, sent_ref, out_ref):
    rows, width = kv0_ref.shape[1], kv0_ref.shape[1] // 2
    ids0 = kv0_ref[rows : rows + 1, :].astype(jnp.float32)
    first = ids0[:, 0:1]
    height = heads * width + pad
    start = pl.multiple_of((1 - core()) * height, pad)
    theirs = sent_ref.at[pl.ds(start, height), :]
    extra = theirs[heads * width :, :].astype(jnp.float32)
    usable = (ids0 == first) & (extra[3 * heads : 3 * heads + 1, :] == first)
    for head in range(heads):
        lse = lse_ref[head : head + 1, :]
        their = (
            extra[3 * head : 3 * head + 1, :]
            + extra[3 * head + 1 : 3 * head + 2, :]
            + extra[3 * head + 2 : 3 * head + 3, :]
        )
        their = jnp.where(usable, their, lowest)
        high = jnp.maximum(lse, their)
        a = jnp.exp2(lse - high)
        b = jnp.exp2(their - high)
        share = 1.0 / (a + b)
        place = slice(head * width, (head + 1) * width)
        merged = mean_ref[place, :] * (a * share) + theirs[place, :].astype(jnp.float32) * (b * share)
        out_ref[:, place] = merged.T.astype(jnp.bfloat16)


def call(kernel, outs, flops, *args):
    vmem = pl.BlockSpec(memory_space=pltpu.VMEM)
    moved = sum(math.prod(a.shape) * a.dtype.itemsize for a in (*args, *outs))
    return pl.pallas_call(
        kernel,
        out_shape=outs,
        in_specs=[vmem] * len(args),
        out_specs=[vmem] * len(outs),
        cost_estimate=pl.CostEstimate(flops=flops, bytes_accessed=moved, transcendentals=flops // 512),
        compiler_params=pltpu.CompilerParams(vmem_limit_bytes=40 * 2**20),
    )(*args)


def body(queries, keys, values, doc_ids):
    rows, width = keys.shape
    heads = queries.shape[1] // width
    scale = math.log2(math.e) / math.sqrt(width)
    ids = jnp.broadcast_to(doc_ids.astype(jnp.bfloat16)[None, :], (pad, rows))
    kv0 = jnp.concatenate([jnp.concatenate([keys, values], axis=1), ids], axis=0)
    kv4 = chips_on(kv0, 4)
    kv1 = chips_on(kv0, 1)
    kv2 = chips_on(kv0, 2)
    kv3 = chips_on(kv4, -1)
    q_chip = both_cores(queries)
    f32, bf16 = jnp.float32, jnp.bfloat16
    unit = 4 * heads * rows * rows * width
    stat, acc = call(
        functools.partial(early_kernel, scale, heads),
        [
            jax.ShapeDtypeStruct((4 * heads, rows), f32),
            jax.ShapeDtypeStruct((2 * heads * width, rows), f32),
        ],
        6 * unit,
        q_chip,
        kv0,
        kv1,
        kv4,
    )
    lse, mean, send = call(
        functools.partial(late_kernel, scale, heads),
        [
            jax.ShapeDtypeStruct((8, rows), f32),
            jax.ShapeDtypeStruct((heads * width, rows), f32),
            jax.ShapeDtypeStruct((heads * width + pad, rows), bf16),
        ],
        4 * unit,
        q_chip,
        kv0,
        kv1,
        kv2,
        kv3,
        stat,
        acc,
    )
    sent = both_cores(send)
    (out,) = call(
        functools.partial(merge_kernel, heads),
        [jax.ShapeDtypeStruct((rows, heads * width), bf16)],
        unit // 64,
        kv0,
        lse,
        mean,
        sent,
    )
    return out


def solution(mesh):
    split_spec = P(axes, None)
    return jax.shard_map(
        body,
        mesh=mesh,
        in_specs=(split_spec, split_spec, split_spec, P(axes)),
        out_specs=split_spec,
        check_vma=False,
    )
```

time: 186 us -> 35.6 us (0.19)
  the two profiles are of different devices: /device:TPU:35 before, /device:TPU:1 now
where the time goes in v1:
time: 35.6 us; the launch traced here: 35.4 us
  starting transfers between devices  14.6 us (41%)
  Pallas kernels  7.7 us (22%)
  waiting for transfers between devices  6.09 us (17%)
  blocking collectives  5.37 us (15%)
  other arithmetic  1.61 us (5%)
    ppermute x4, starting transfers between devices, chips_on(): lax.ppermute(value, axes, [(d, (d + shift) % count) for d in range(count)])  14.6 us
    pallas_call x3, Pallas kernels, call(): pl.pallas_call(kernel, out_shape=outs, in_specs=[vmem] * len(args), out_s...  7.7 us
    ppermute x4, waiting for transfers between devices, chips_on(): lax.ppermute(value, axes, [(d, (d + shift) % count) for d in range(count)])  6.09 us
    all_gather x2, blocking collectives, both_cores(): lax.all_gather(value, 'context', axis=0, tiled=True, axis_index_groups=pa...  5.37 us
    concatenate x1, other arithmetic, body(): jnp.concatenate([jnp.concatenate([keys, values], axis=1), ids], axis=0)  0.89 us
    convert_element_type x1, other arithmetic, body(): ids = jnp.broadcast_to(doc_ids.astype(jnp.bfloat16)[None, :], (pad, rows))  0.73 us
  transfers between devices with their start and end apart: 4, of which 1 were waited for; matrix products, arithmetic and copies ran while one was open for 0% of the time, Pallas kernels for 11%

profile of v1, /device:TPU:1, one launch (start us, length us, event | category | flops | bytes accessed | tf_op | source)
XLA Modules:
  0.0 35.4 jit_solution(10918018066567684851)
XLA Ops:
  0.0 0.0 copy-start
  0.0 0.7 %convert_element_type.3 = bf16[256]{0:T(256)(128)(2,1)S(1)} convert(s32[256]{0:T(256)} %param.7) | non-fusion elementwise | flops 256 | bytes 1536 | tf_op jit(solution)/shard_map/convert_element_type | solution.py:214
  0.7 0.9 %pad_maximum_fusion.kv0_ref = bf16[272,256]{1,0:T(8,128)(2,1)S(1)} fusion(bf16[16,256]{1,0:T(8,128)(2,1)S(1)} %broadcast_in_dim.2, bf16[256,128]{1,0:T(8,128)(2,1)} %param.6, bf16[256,128]{1,0:T(8,128)(2,1)} %param.5), kind=kLoop, calls=%fused_computation | loop fusion | flops 417792 | bytes 278528 | tf_op jit(solution)/shard_map/concatenate | solution.py:215
  1.6 7.8 %collective-permute-start.2 = (bf16[272,256]{1,0:T(8,128)(2,1)S(1)}, bf16[272,256]{1,0:T(8,128)(2,1)S(1)}, u32[]{:S(2)}, u32[]{:S(2)}) collective-permute-start(bf16[272,256]{1,0:T(8,128)(2,1)S(1)} %pad_maximum_fusion.kv0_ref), channel_id=1, source_target_pairs={{0,8},{1,9},{2,10},{3,11},{4,12},{5,13},{6,14},{7,15},{8,16},{9,17... | collective-permute-start | bytes 417800 | tf_op jit(solution)/shard_map/ppermute | solution.py:20
  9.4 0.7 %collective-permute-start = (bf16[272,256]{1,0:T(8,128)(2,1)S(1)}, bf16[272,256]{1,0:T(8,128)(2,1)S(1)}, u32[]{:S(2)}, u32[]{:S(2)}) collective-permute-start(bf16[272,256]{1,0:T(8,128)(2,1)S(1)} %pad_maximum_fusion.kv0_ref), channel_id=1, source_target_pairs={{0,2},{1,3},{2,4},{3,5},{4,6},{5,7},{6,8},{7,9},{8,10},{9,11},{10,... | collective-permute-start | bytes 417800 | tf_op jit(solution)/shard_map/ppermute | solution.py:20
  10.2 1.2 %collective-permute-start.1 = (bf16[272,256]{1,0:T(8,128)(2,1)S(1)}, bf16[272,256]{1,0:T(8,128)(2,1)S(1)}, u32[]{:S(2)}, u32[]{:S(2)}) collective-permute-start(bf16[272,256]{1,0:T(8,128)(2,1)S(1)} %pad_maximum_fusion.kv0_ref), channel_id=1, source_target_pairs={{0,4},{1,5},{2,6},{3,7},{4,8},{5,9},{6,10},{7,11},{8,12},{9,13},{1... | collective-permute-start | bytes 417800 | tf_op jit(solution)/shard_map/ppermute | solution.py:20
  11.4 6.1 %collective-permute-done.2.kv4_ref = bf16[272,256]{1,0:T(8,128)(2,1)S(1)} collective-permute-done((bf16[272,256]{1,0:T(8,128)(2,1)S(1)}, bf16[272,256]{1,0:T(8,128)(2,1)S(1)}, u32[]{:S(2)}, u32[]{:S(2)}) %collective-permute-start.2) | collective-permute-done | bytes 139296 | tf_op jit(solution)/shard_map/ppermute | solution.py:20
  17.5 4.8 %collective-permute-start.3 = (bf16[272,256]{1,0:T(8,128)(2,1)S(1)}, bf16[272,256]{1,0:T(8,128)(2,1)S(1)}, u32[]{:S(2)}, u32[]{:S(2)}) collective-permute-start(bf16[272,256]{1,0:T(8,128)(2,1)S(1)} %collective-permute-done.2.kv4_ref), channel_id=1, source_target_pairs={{0,254},{1,255},{2,0},{3,1},{4,2},{5,3},{6,4},{7,5},{8,6},{9,7},{1... | collective-permute-start | bytes 417800 | tf_op jit(solution)/shard_map/ppermute | solution.py:20
  22.3 0.0 copy-done
  22.3 3.2 %all_gather.6.q_ref = bf16[512,512]{1,0:T(8,128)(2,1)S(1)} all-gather(bf16[256,512]{1,0:T(8,128)(2,1)S(1)} %copy-done), channel_id=1, replica_groups={{0,1},{2,3},{4,5},{6,7},{8,9},{10,11},{12,13},{14,15},{16,17},{18,19},{..., dimensions={0}, use_global_device_ids=true | all-gather | bytes 786432 | tf_op jit(solution)/shard_map/all_gather | solution.py:26
  25.5 0.0 collective-permute-done.kv1_ref
  25.5 3.8 %shard_map.46 = (f32[16,256]{1,0:T(8,128)S(1)}, f32[1024,256]{1,0:T(8,128)S(1)}) custom-call(bf16[512,512]{1,0:T(8,128)(2,1)S(1)} %all_gather.6.q_ref, bf16[272,256]{1,0:T(8,128)(2,1)S(1)} %pad_maximum_fusion.kv0_ref, bf16[272,256]{1,0:T(8,128)(2,1)S(1)} %collective-permute-done.kv1_ref, bf16[272,256]{1,0:T(8,128)(2,1)S(1)} %collective-permute-done.2.kv4_ref), custom_call_target="tpu_custom_call" | custom-call | flops 805306368 | bytes 2007040 | tf_op jit(solution)/shard_map/pallas_call | solution.py:200
  29.2 0.0 collective-permute-done.1.kv2_ref
  29.3 0.0 collective-permute-done.3.kv3_ref
  29.3 3.0 %shard_map.47 = (f32[8,256]{1,0:T(8,128)S(1)}, f32[512,256]{1,0:T(8,128)S(1)}, bf16[528,256]{1,0:T(8,128)(2,1)S(1)}) custom-call(bf16[512,512]{1,0:T(8,128)(2,1)S(1)} %all_gather.6.q_ref, bf16[272,256]{1,0:T(8,128)(2,1)S(1)} %pad_maximum_fusion.kv0_ref, bf16[272,256]{1,0:T(8,128)(2,1)S(1)} %collective-permute-done.kv1_ref, ...), custom_call_target="tpu_custom_call" | custom-call | flops 536870912 | bytes 2949120 | tf_op jit(solution)/shard_map/pallas_call | solution.py:200
  32.3 2.2 %all_gather.7.sent_ref = bf16[1056,256]{1,0:T(8,128)(2,1)S(1)} all-gather(bf16[528,256]{1,0:T(8,128)(2,1)S(1)} %get-tuple-element.14), channel_id=1, replica_groups={{0,1},{2,3},{4,5},{6,7},{8,9},{10,11},{12,13},{14,15},{16,17},{18,19},{..., dimensions={0}, use_global_device_ids=true | all-gather | bytes 811008 | tf_op jit(solution)/shard_map/all_gather | solution.py:26
  34.5 1.0 %shard_map.48 = bf16[256,512]{1,0:T(8,128)(2,1)} custom-call(bf16[272,256]{1,0:T(8,128)(2,1)S(1)} %pad_maximum_fusion.kv0_ref, f32[8,256]{1,0:T(8,128)S(1)} %get-tuple-element.12.lse_ref, f32[512,256]{1,0:T(8,128)S(1)} %get-tuple-element.13.mean_ref, bf16[1056,256]{1,0:T(8,128)(2,1)S(1)} %all_gather.7.sent_ref), custom_call_target="tpu_custom_call" | custom-call | flops 2097152 | bytes 1474560 | tf_op jit(solution)/shard_map/pallas_call | solution.py:200
  (1 shorter events, 0.0 us)
Async XLA Ops:
  0.0 22.3 %copy-start = (bf16[256,512]{1,0:T(8,128)(2,1)S(1)}, bf16[256,512]{1,0:T(8,128)(2,1)}, u32[]{:S(2)}) copy-start(bf16[256,512]{1,0:T(8,128)(2,1)} %param.4) | copy-start | bytes 786436
  1.6 15.8 %collective-permute-start.2 = (bf16[272,256]{1,0:T(8,128)(2,1)S(1)}, bf16[272,256]{1,0:T(8,128)(2,1)S(1)}, u32[]{:S(2)}, u32[]{:S(2)}) collective-permute-start(bf16[272,256]{1,0:T(8,128)(2,1)S(1)} %pad_maximum_fusion.kv0_ref), channel_id=1, source_target_pairs={{0,8},{1,9},{2,10},{3,11},{4,12},{5,13},{6,14},{7,15},{8,16},{9,17... | collective-permute-start | bytes 417800 | tf_op jit(solution)/shard_map/ppermute | solution.py:20
  9.4 16.0 %collective-permute-start = (bf16[272,256]{1,0:T(8,128)(2,1)S(1)}, bf16[272,256]{1,0:T(8,128)(2,1)S(1)}, u32[]{:S(2)}, u32[]{:S(2)}) collective-permute-start(bf16[272,256]{1,0:T(8,128)(2,1)S(1)} %pad_maximum_fusion.kv0_ref), channel_id=1, source_target_pairs={{0,2},{1,3},{2,4},{3,5},{4,6},{5,7},{6,8},{7,9},{8,10},{9,11},{10,... | collective-permute-start | bytes 417800 | tf_op jit(solution)/shard_map/ppermute | solution.py:20
  10.2 19.1 %collective-permute-start.1 = (bf16[272,256]{1,0:T(8,128)(2,1)S(1)}, bf16[272,256]{1,0:T(8,128)(2,1)S(1)}, u32[]{:S(2)}, u32[]{:S(2)}) collective-permute-start(bf16[272,256]{1,0:T(8,128)(2,1)S(1)} %pad_maximum_fusion.kv0_ref), channel_id=1, source_target_pairs={{0,4},{1,5},{2,6},{3,7},{4,8},{5,9},{6,10},{7,11},{8,12},{9,13},{1... | collective-permute-start | bytes 417800 | tf_op jit(solution)/shard_map/ppermute | solution.py:20
  17.5 11.8 %collective-permute-start.3 = (bf16[272,256]{1,0:T(8,128)(2,1)S(1)}, bf16[272,256]{1,0:T(8,128)(2,1)S(1)}, u32[]{:S(2)}, u32[]{:S(2)}) collective-permute-start(bf16[272,256]{1,0:T(8,128)(2,1)S(1)} %collective-permute-done.2.kv4_ref), channel_id=1, source_target_pairs={{0,254},{1,255},{2,0},{3,1},{4,2},{5,3},{6,4},{7,5},{8,6},{9,7},{1... | collective-permute-start | bytes 417800 | tf_op jit(solution)/shard_map/ppermute | solution.py:20

commit v2 on v0

v2 whole, which is shorter than its diff:
```python
import functools
import math

import jax
import jax.numpy as jnp
from jax import lax
from jax.experimental import pallas as pl
from jax.experimental.pallas import tpu as pltpu
from jax.sharding import PartitionSpec as P

outside = -1e30
axes = ("dp", "context")
pad = 8


def chips_on(value, steps, wrap):
    count = lax.axis_size(axes[0]) * lax.axis_size(axes[1])
    shift = 2 * steps
    pairs = [(d, (d + shift) % count) for d in range(count)]
    return lax.ppermute(value, axes, [(a, b) for a, b in pairs if wrap or b == a + shift])


def other_core(value):
    count = lax.axis_size(axes[0]) * lax.axis_size(axes[1])
    return lax.ppermute(value, axes, [(d, d ^ 1) for d in range(count)])


def pack(keys, values, doc_ids):
    rows = keys.shape[0]
    packed = jnp.pad(jnp.concatenate([keys, values], axis=1), ((0, pad), (0, 0)))
    packed, doc_ids = lax.optimization_barrier((packed, doc_ids))
    ids = jnp.broadcast_to((doc_ids + 1).astype(jnp.bfloat16)[None, :], (pad, rows))
    return lax.dynamic_update_slice(packed, ids, (rows, 0))


def nt(a, b):
    return lax.dot_general(a, b, (((1,), (1,)), ((), ())), preferred_element_type=jnp.float32)


def nn(a, b):
    return lax.dot_general(a, b, (((1,), (0,)), ((), ())), preferred_element_type=jnp.float32)


def iotas(rows, columns):
    down = lax.broadcasted_iota(jnp.int32, (rows, columns), 0)
    across = lax.broadcasted_iota(jnp.int32, (rows, columns), 1)
    return down, across


def ids_of(ref):
    rows = ref.shape[1]
    return ref[rows : rows + 1, :].astype(jnp.float32)


def count(ids, wanted):
    return jnp.sum(jnp.where(ids == wanted, 1.0, 0.0), axis=1, keepdims=True)


def on_core_one():
    return jnp.where(lax.rem(lax.axis_index("context"), 2) == 1, 1.0, 0.0)


def causal_mask(own_ref):
    rows = own_ref.shape[1]
    ids = ids_of(own_ref)
    at_row, at_key = iotas(rows, rows)
    ids_col = jnp.sum(jnp.where(at_key == at_row, ids, 0.0), axis=1, keepdims=True)
    return (ids_col == ids) & (at_key <= at_row)


def wide_keys(ref, first, keep):
    rows, width = ref.shape[1], ref.shape[1] // 2
    matches = count(ids_of(ref), first) * keep
    down, across = iotas(rows, width)
    masked = jnp.where(down.astype(jnp.float32) >= rows - matches, 0.0, outside)
    extra = jnp.where(across == 0, masked, jnp.where(across == 1, 1.0, 0.0))
    return jnp.concatenate([ref[0:rows, 0:width], extra.astype(jnp.bfloat16)], axis=1)


def wide_values(ref):
    rows, width = ref.shape[1], ref.shape[1] // 2
    return jnp.concatenate([ref[0:rows, width : 2 * width], jnp.ones((rows, width), jnp.bfloat16)], axis=1)


def query_extra(ids, first, rows, width):
    down, across = iotas(rows, width)
    in_first = jnp.where(down.astype(jnp.float32) < count(ids, first), 0.0, outside)
    return jnp.where(across == 0, 1.0, jnp.where(across == 1, in_first, 0.0)).astype(jnp.bfloat16)


def attend_kernel(scale, heads, begin, end, n_pieces, q_ref, own_ref, *refs):
    rows, width = own_ref.shape[1], own_ref.shape[1] // 2
    piece_refs, refs = refs[:n_pieces], refs[n_pieces:]
    if begin:
        q_out, top_out, acc_out, keys_ref, values_ref = refs
    elif end:
        top_in, acc_in, out_ref, keys_ref, values_ref, done_ref, sems = refs
    else:
        top_in, acc_in, top_out, acc_out, keys_ref, values_ref = refs
    ids = ids_of(own_ref)
    first = ids[:, 0:1]
    if begin:
        causal = causal_mask(own_ref)
        own_keys, own_values = own_ref[0:rows, 0:width], wide_values(own_ref)
        extra = query_extra(ids, first, rows, width)
    for at, ref in enumerate(piece_refs):
        here = slice(at * rows, (at + 1) * rows)
        keys_ref[here, :] = wide_keys(ref, first, on_core_one() if begin and at == 0 else 1.0)
        values_ref[here, :] = wide_values(ref)
    copies = []
    for head in range(heads):
        here = slice(head * rows, (head + 1) * rows)
        place = slice(head * width, (head + 1) * width)
        if begin:
            q = q_ref[:, place]
            wide = jnp.concatenate([q, extra], axis=1)
            q_out[here, :] = wide
            own_scores = jnp.where(causal, nt(q, own_keys), outside)
            before = jnp.max(own_scores, axis=1, keepdims=True)
        else:
            wide = q_ref[here, :]
            before = top_in[here, 0:1]
        scores = nt(wide, keys_ref[...])
        top = jnp.maximum(before, jnp.max(scores, axis=1, keepdims=True))
        acc = nn(jnp.exp2((scores - top) * scale).astype(jnp.bfloat16), values_ref[...])
        if begin:
            acc = acc + nn(jnp.exp2((own_scores - top) * scale).astype(jnp.bfloat16), own_values)
        else:
            acc = acc + acc_in[here, :] * jnp.exp2((before - top) * scale)
        if end:
            done_ref[:, place] = (acc[:, 0:width] / acc[:, width:]).astype(jnp.bfloat16)
            copy = pltpu.make_async_copy(done_ref.at[:, place], out_ref.at[:, place], sems.at[head])
            copy.start()
            copies.append(copy)
        else:
            top_out[here, :] = jnp.broadcast_to(top, (rows, width))
            acc_out[here, :] = acc
    for copy in copies:
        copy.wait()


def call(scale, heads, begin, end, q, own, pieces, state):
    vmem = pl.BlockSpec(memory_space=pltpu.VMEM)
    rows, width = own.shape[1], own.shape[1] // 2
    shape, f32, bf16 = jax.ShapeDtypeStruct, jnp.float32, jnp.bfloat16
    outs = [shape((heads * rows, width), f32), shape((heads * rows, 2 * width), f32)]
    if begin:
        outs.insert(0, shape((heads * rows, 2 * width), bf16))
    scratch = [pltpu.VMEM((len(pieces) * rows, 2 * width), bf16)] * 2
    out_specs = [vmem] * len(outs)
    if end:
        outs, out_specs = [shape((rows, heads * width), bf16)], [pl.BlockSpec(memory_space=pl.ANY)]
        scratch += [pltpu.VMEM((rows, heads * width), bf16), pltpu.SemaphoreType.DMA((heads,))]
    args = (q, own, *pieces, *state)
    moved = sum(math.prod(a.shape) * a.dtype.itemsize for a in (*args, *outs))
    flops = 8 * (len(pieces) + begin) * heads * rows * rows * width
    return pl.pallas_call(
        functools.partial(attend_kernel, scale, heads, begin, end, len(pieces)),
        out_shape=outs,
        in_specs=[vmem] * len(args),
        out_specs=out_specs,
        scratch_shapes=scratch,
        cost_estimate=pl.CostEstimate(flops=flops, bytes_accessed=moved, transcendentals=flops // 512),
        compiler_params=pltpu.CompilerParams(vmem_limit_bytes=40 * 2**20),
    )(*args)


def body(queries, keys, values, doc_ids):
    heads = queries.shape[1] // keys.shape[1]
    scale = math.log2(math.e) / math.sqrt(keys.shape[1])
    kv0 = pack(keys, values, doc_ids)
    kv4 = chips_on(kv0, 4, True)
    kv2 = chips_on(kv0, 2, False)
    kv1 = chips_on(kv0, 1, False)
    kv3 = chips_on(kv4, -1, True)
    attend = functools.partial(call, scale, heads)

    def both(piece):
        return [piece, other_core(piece)]

    kv4t = other_core(kv4)
    q, *state = attend(True, False, queries, kv0, [other_core(kv0), kv4], [])
    q, state, kv1 = lax.optimization_barrier((q, state, kv1))
    state = attend(False, False, q, kv0, [*both(kv1), kv4t], state)
    (out,) = attend(False, True, q, kv0, [*both(kv2), *both(kv3)], state)
    return out


def solution(mesh):
    split_spec = P(axes, None)
    return jax.shard_map(
        body,
        mesh=mesh,
        in_specs=(split_spec, split_spec, split_spec, P(axes)),
        out_specs=split_spec,
        check_vma=False,
    )
```

time: 186 us -> 31.3 us (0.17); the launches traced: 184 us -> 31.1 us
  waiting for transfers between devices: 70.5 us -> 8.76 us
  blocking collectives: 36.4 us -> 0 us
  matrix products: 30.8 us -> 0 us
  other arithmetic: 21.5 us -> 0.94 us
  between operations: 13.3 us -> 0.1 us
  starting transfers between devices: 7.61 us -> 15.3 us
  Pallas kernels: 0 us -> 6.02 us
  local copies, waits for them, and re-layouts: 3.68 us -> 0.01 us
    all_gather x4 -> x0, waiting for transfers between devices: 65.6 us -> none  [the longest x1 30.4 us: body(): lax.all_gather(prior[1], 'context', axis=0, tiled=True)]
    all_gather x2 -> x0, blocking collectives: 36.4 us -> none  [the longest x1 20.1 us: body(): lax.all_gather(query_ids, 'context', axis=0, tiled=True)]
    dot_general x4 -> x0, matrix products: 30.8 us -> none  [the longest x2 18.4 us: attend(): jnp.einsum('hqk,kd->hqd', raised.astype(jnp.bfloat16), value_block, prefe...]
    reduce_sum x1 -> x0, other arithmetic: 16 us -> none  [attend(): total = total * fade + jnp.sum(raised, axis=-1)]
    ppermute x3 -> x9, starting transfers between devices: 7.49 us -> 15.3 us  [the longest x4 12.6 us: chips_on(): lax.ppermute(value, axes, [(a, b) for a, b in pairs if wrap or b == a + s...]
    pallas_call x0 -> x3, Pallas kernels: none -> 6.02 us  [call(): pl.pallas_call(functools.partial(attend_kernel, scale, heads, begin, end,...]
    and x1 -> x0, other arithmetic: 4.66 us -> none  [attend(): (query_ids[:, None] == key_docs[None, :]) & (key_pos[None, :] <= query_po...]
    ppermute x3 -> x9, waiting for transfers between devices: 4.12 us -> 8.76 us  [the longest x4 8.75 us: chips_on(): lax.ppermute(value, axes, [(a, b) for a, b in pairs if wrap or b == a + s...]
  transfers between devices with their start and end apart: 7 -> 9, of which waited for: 4 -> 2; matrix products, arithmetic and copies ran while one was open for 24% -> 0% of each run, Pallas kernels for 0% -> 10%
where the time goes in v2:
time: 31.3 us; the launch traced here: 31.1 us
  starting transfers between devices  15.3 us (49%)
  waiting for transfers between devices  8.76 us (28%)
  Pallas kernels  6.02 us (19%)
  other arithmetic  0.94 us (3%)
    ppermute x4, starting transfers between devices, chips_on(): lax.ppermute(value, axes, [(a, b) for a, b in pairs if wrap or b == a + s...  12.6 us
    ppermute x4, waiting for transfers between devices, chips_on(): lax.ppermute(value, axes, [(a, b) for a, b in pairs if wrap or b == a + s...  8.75 us
    pallas_call x3, Pallas kernels, call(): pl.pallas_call(functools.partial(attend_kernel, scale, heads, begin, end,...  6.02 us
    ppermute x5, starting transfers between devices, other_core(): return lax.ppermute(value, axes, [(d, d ^ 1) for d in range(count)])  2.66 us
    concatenate x1, other arithmetic, pack(): jnp.concatenate([keys, values], axis=1)  0.93 us
  transfers between devices with their start and end apart: 9, of which 2 were waited for; matrix products, arithmetic and copies ran while one was open for 0% of the time, Pallas kernels for 10%

profile of v2, /device:TPU:35, one launch (start us, length us, event | category | flops | bytes accessed | tf_op | source)
XLA Modules:
  0.0 31.1 jit_solution(8165394418064614887)
XLA Ops:
  0.0 0.9 %fusion.2 = bf16[264,256]{1,0:T(8,128)(2,1)S(1)} fusion(bf16[256,128]{1,0:T(8,128)(2,1)} %param.6, bf16[256,128]{1,0:T(8,128)(2,1)} %param.5), kind=kLoop, calls=%fused_computation.3 | loop fusion | flops 473088 | bytes 266240 | tf_op jit(solution)/shard_map/concatenate | solution.py:30
  0.9 0.0 copy-done.1
  1.0 6.1 %collective-permute-start.1 = (bf16[264,256]{1,0:T(8,128)(2,1)S(1)}, bf16[264,256]{1,0:T(8,128)(2,1)S(1)}, u32[]{:S(2)}, u32[]{:S(2)}) collective-permute-start(bf16[264,256]{1,0:T(8,128)(2,1)S(1)} %broadcast_dynamic-update-slice_fusion.own_ref), channel_id=1, source_target_pairs={{0,8},{1,9},{2,10},{3,11},{4,12},{5,13},{6,14},{7,15},{8,16},{9,17... | collective-permute-start | bytes 405512 | tf_op jit(solution)/shard_map/ppermute | solution.py:20
  7.1 1.0 %collective-permute-start = (bf16[264,256]{1,0:T(8,128)(2,1)S(1)}, bf16[264,256]{1,0:T(8,128)(2,1)S(1)}, u32[]{:S(2)}, u32[]{:S(2)}) collective-permute-start(bf16[264,256]{1,0:T(8,128)(2,1)S(1)} %broadcast_dynamic-update-slice_fusion.own_ref), channel_id=1, source_target_pairs={{0,1},{1,0},{2,3},{3,2},{4,5},{5,4},{6,7},{7,6},{8,9},{9,8},{10,11... | collective-permute-start | bytes 405512 | tf_op jit(solution)/shard_map/ppermute | solution.py:25
  8.0 2.6 %collective-permute-start.2 = (bf16[264,256]{1,0:T(8,128)(2,1)S(1)}, bf16[264,256]{1,0:T(8,128)(2,1)S(1)}, u32[]{:S(2)}, u32[]{:S(2)}) collective-permute-start(bf16[264,256]{1,0:T(8,128)(2,1)S(1)} %broadcast_dynamic-update-slice_fusion.own_ref), channel_id=1, source_target_pairs={{0,2},{1,3},{2,4},{3,5},{4,6},{5,7},{6,8},{7,9},{8,10},{9,11},{10,... | collective-permute-start | bytes 405512 | tf_op jit(solution)/shard_map/ppermute | solution.py:20
  10.7 2.4 %collective-permute-start.3 = (bf16[264,256]{1,0:T(8,128)(2,1)S(1)}, bf16[264,256]{1,0:T(8,128)(2,1)S(1)}, u32[]{:S(2)}, u32[]{:S(2)}) collective-permute-start(bf16[264,256]{1,0:T(8,128)(2,1)S(1)} %broadcast_dynamic-update-slice_fusion.own_ref), channel_id=1, source_target_pairs={{0,4},{1,5},{2,6},{3,7},{4,8},{5,9},{6,10},{7,11},{8,12},{9,13},{1... | collective-permute-start | bytes 405512 | tf_op jit(solution)/shard_map/ppermute | solution.py:20
  13.0 0.0 collective-permute-done.1.refs_1_
  13.1 1.5 %collective-permute-start.5 = (bf16[264,256]{1,0:T(8,128)(2,1)S(1)}, bf16[264,256]{1,0:T(8,128)(2,1)S(1)}, u32[]{:S(2)}, u32[]{:S(2)}) collective-permute-start(bf16[264,256]{1,0:T(8,128)(2,1)S(1)} %collective-permute-done.1.refs_1_), channel_id=1, source_target_pairs={{0,254},{1,255},{2,0},{3,1},{4,2},{5,3},{6,4},{7,5},{8,6},{9,7},{1... | collective-permute-start | bytes 405512 | tf_op jit(solution)/shard_map/ppermute | solution.py:20
  14.6 0.0 collective-permute-done.refs_0_
  14.6 0.0 copy-done
  14.6 1.5 %shard_map.46 = (bf16[1024,256]{1,0:T(8,128)(2,1)S(1)}, f32[1024,128]{1,0:T(8,128)S(1)}, f32[1024,256]{1,0:T(8,128)S(1)}) custom-call(bf16[256,512]{1,0:T(8,128)(2,1)S(1)} %copy-done, bf16[264,256]{1,0:T(8,128)(2,1)S(1)} %broadcast_dynamic-update-slice_fusion.own_ref, bf16[264,256]{1,0:T(8,128)(2,1)S(1)} %collective-permute-done.refs_0_, ...), custom_call_target="tpu_custom_call" | custom-call | flops 805306368 | bytes 2764800 | tf_op jit(solution)/shard_map/pallas_call | solution.py:157
  16.1 1.5 %collective-permute-done.2.refs_0_ = bf16[264,256]{1,0:T(8,128)(2,1)S(1)} collective-permute-done((bf16[264,256]{1,0:T(8,128)(2,1)S(1)}, bf16[264,256]{1,0:T(8,128)(2,1)S(1)}, u32[]{:S(2)}, u32[]{:S(2)}) %collective-permute-start.2) | collective-permute-done | bytes 135200 | tf_op jit(solution)/shard_map/ppermute | solution.py:20
  17.6 0.7 %collective-permute-start.7 = (bf16[264,256]{1,0:T(8,128)(2,1)S(1)}, bf16[264,256]{1,0:T(8,128)(2,1)S(1)}, u32[]{:S(2)}, u32[]{:S(2)}) collective-permute-start(bf16[264,256]{1,0:T(8,128)(2,1)S(1)} %collective-permute-done.2.refs_0_), channel_id=1, source_target_pairs={{0,1},{1,0},{2,3},{3,2},{4,5},{5,4},{6,7},{7,6},{8,9},{9,8},{10,11... | collective-permute-start | bytes 405512 | tf_op jit(solution)/shard_map/ppermute | solution.py:25
  18.3 0.1 collective-permute-start.8
  18.4 7.2 %collective-permute-done.3.refs_0_ = bf16[264,256]{1,0:T(8,128)(2,1)S(1)} collective-permute-done((bf16[264,256]{1,0:T(8,128)(2,1)S(1)}, bf16[264,256]{1,0:T(8,128)(2,1)S(1)}, u32[]{:S(2)}, u32[]{:S(2)}) %collective-permute-start.3) | collective-permute-done | bytes 135200 | tf_op jit(solution)/shard_map/ppermute | solution.py:20
  25.7 0.9 %collective-permute-start.4 = (bf16[264,256]{1,0:T(8,128)(2,1)S(1)}, bf16[264,256]{1,0:T(8,128)(2,1)S(1)}, u32[]{:S(2)}, u32[]{:S(2)}) collective-permute-start(bf16[264,256]{1,0:T(8,128)(2,1)S(1)} %collective-permute-done.3.refs_0_), channel_id=1, source_target_pairs={{0,1},{1,0},{2,3},{3,2},{4,5},{5,4},{6,7},{7,6},{8,9},{9,8},{10,11... | collective-permute-start | bytes 405512 | tf_op jit(solution)/shard_map/ppermute | solution.py:25
  26.6 0.0 collective-permute-done.5.refs_2_
  26.6 0.0 collective-permute-start.6
  26.6 0.0 collective-permute-done.7.refs_1_
  26.6 0.0 collective-permute-done.8.refs_2_
  26.6 1.7 %shard_map.47 = (f32[1024,128]{1,0:T(8,128)S(1)}, f32[1024,256]{1,0:T(8,128)S(1)}) custom-call(bf16[1024,256]{1,0:T(8,128)(2,1)S(1)} %get-tuple-element.21.q_ref, bf16[264,256]{1,0:T(8,128)(2,1)S(1)} %broadcast_dynamic-update-slice_fusion.own_ref, bf16[264,256]{1,0:T(8,128)(2,1)S(1)} %collective-permute-done.2.refs_0_, ...), custom_call_target="tpu_custom_call" | custom-call | flops 805306368 | bytes 4210688 | tf_op jit(solution)/shard_map/pallas_call | solution.py:157
  28.3 0.0 collective-permute-done.4.refs_1_
  28.3 0.0 collective-permute-done.6.refs_3_
  28.3 2.8 %shard_map.48 = bf16[256,512]{1,0:T(8,128)(2,1)} custom-call(bf16[1024,256]{1,0:T(8,128)(2,1)S(1)} %get-tuple-element.21.q_ref, bf16[264,256]{1,0:T(8,128)(2,1)S(1)} %broadcast_dynamic-update-slice_fusion.own_ref, bf16[264,256]{1,0:T(8,128)(2,1)S(1)} %collective-permute-done.3.refs_0_, bf16[264,256]{1,0:T(8,128)(2,1)S(1)} %collective-permute-done.4.refs_1_, ...), custom_call_target="tpu_custom_call" | custom-call | flops 1073741824 | bytes 3035136 | tf_op jit(solution)/shard_map/pallas_call | solution.py:157
  (4 shorter events, 0.0 us)
Async XLA Ops:
  0.0 0.9 %copy-start.1 = (s32[256]{0:T(256)S(1)}, s32[256]{0:T(256)}, u32[]{:S(2)}) copy-start(s32[256]{0:T(256)} %param.7) | copy-start | bytes 3076
  0.0 14.6 %copy-start = (bf16[256,512]{1,0:T(8,128)(2,1)S(1)}, bf16[256,512]{1,0:T(8,128)(2,1)}, u32[]{:S(2)}) copy-start(bf16[256,512]{1,0:T(8,128)(2,1)} %q_ref.1) | copy-start | bytes 786436
  1.0 12.1 %collective-permute-start.1 = (bf16[264,256]{1,0:T(8,128)(2,1)S(1)}, bf16[264,256]{1,0:T(8,128)(2,1)S(1)}, u32[]{:S(2)}, u32[]{:S(2)}) collective-permute-start(bf16[264,256]{1,0:T(8,128)(2,1)S(1)} %broadcast_dynamic-update-slice_fusion.own_ref), channel_id=1, source_target_pairs={{0,8},{1,9},{2,10},{3,11},{4,12},{5,13},{6,14},{7,15},{8,16},{9,17... | collective-permute-start | bytes 405512 | tf_op jit(solution)/shard_map/ppermute | solution.py:20
  7.1 7.5 %collective-permute-start = (bf16[264,256]{1,0:T(8,128)(2,1)S(1)}, bf16[264,256]{1,0:T(8,128)(2,1)S(1)}, u32[]{:S(2)}, u32[]{:S(2)}) collective-permute-start(bf16[264,256]{1,0:T(8,128)(2,1)S(1)} %broadcast_dynamic-update-slice_fusion.own_ref), channel_id=1, source_target_pairs={{0,1},{1,0},{2,3},{3,2},{4,5},{5,4},{6,7},{7,6},{8,9},{9,8},{10,11... | collective-permute-start | bytes 405512 | tf_op jit(solution)/shard_map/ppermute | solution.py:25
  8.0 9.6 %collective-permute-start.2 = (bf16[264,256]{1,0:T(8,128)(2,1)S(1)}, bf16[264,256]{1,0:T(8,128)(2,1)S(1)}, u32[]{:S(2)}, u32[]{:S(2)}) collective-permute-start(bf16[264,256]{1,0:T(8,128)(2,1)S(1)} %broadcast_dynamic-update-slice_fusion.own_ref), channel_id=1, source_target_pairs={{0,2},{1,3},{2,4},{3,5},{4,6},{5,7},{6,8},{7,9},{8,10},{9,11},{10,... | collective-permute-start | bytes 405512 | tf_op jit(solution)/shard_map/ppermute | solution.py:20
  10.7 15.0 %collective-permute-start.3 = (bf16[264,256]{1,0:T(8,128)(2,1)S(1)}, bf16[264,256]{1,0:T(8,128)(2,1)S(1)}, u32[]{:S(2)}, u32[]{:S(2)}) collective-permute-start(bf16[264,256]{1,0:T(8,128)(2,1)S(1)} %broadcast_dynamic-update-slice_fusion.own_ref), channel_id=1, source_target_pairs={{0,4},{1,5},{2,6},{3,7},{4,8},{5,9},{6,10},{7,11},{8,12},{9,13},{1... | collective-permute-start | bytes 405512 | tf_op jit(solution)/shard_map/ppermute | solution.py:20
  13.1 13.5 %collective-permute-start.5 = (bf16[264,256]{1,0:T(8,128)(2,1)S(1)}, bf16[264,256]{1,0:T(8,128)(2,1)S(1)}, u32[]{:S(2)}, u32[]{:S(2)}) collective-permute-start(bf16[264,256]{1,0:T(8,128)(2,1)S(1)} %collective-permute-done.1.refs_1_), channel_id=1, source_target_pairs={{0,254},{1,255},{2,0},{3,1},{4,2},{5,3},{6,4},{7,5},{8,6},{9,7},{1... | collective-permute-start | bytes 405512 | tf_op jit(solution)/shard_map/ppermute | solution.py:20
  17.6 8.9 %collective-permute-start.7 = (bf16[264,256]{1,0:T(8,128)(2,1)S(1)}, bf16[264,256]{1,0:T(8,128)(2,1)S(1)}, u32[]{:S(2)}, u32[]{:S(2)}) collective-permute-start(bf16[264,256]{1,0:T(8,128)(2,1)S(1)} %collective-permute-done.2.refs_0_), channel_id=1, source_target_pairs={{0,1},{1,0},{2,3},{3,2},{4,5},{5,4},{6,7},{7,6},{8,9},{9,8},{10,11... | collective-permute-start | bytes 405512 | tf_op jit(solution)/shard_map/ppermute | solution.py:25
  18.3 8.2 %collective-permute-start.8 = (bf16[264,256]{1,0:T(8,128)(2,1)S(1)}, bf16[264,256]{1,0:T(8,128)(2,1)S(1)}, u32[]{:S(2)}, u32[]{:S(2)}) collective-permute-start(bf16[264,256]{1,0:T(8,128)(2,1)S(1)} %collective-permute-done.1.refs_1_), channel_id=1, source_target_pairs={{0,1},{1,0},{2,3},{3,2},{4,5},{5,4},{6,7},{7,6},{8,9},{9,8},{10,11... | collective-permute-start | bytes 405512 | tf_op jit(solution)/shard_map/ppermute | solution.py:25
  25.7 2.6 %collective-permute-start.4 = (bf16[264,256]{1,0:T(8,128)(2,1)S(1)}, bf16[264,256]{1,0:T(8,128)(2,1)S(1)}, u32[]{:S(2)}, u32[]{:S(2)}) collective-permute-start(bf16[264,256]{1,0:T(8,128)(2,1)S(1)} %collective-permute-done.3.refs_0_), channel_id=1, source_target_pairs={{0,1},{1,0},{2,3},{3,2},{4,5},{5,4},{6,7},{7,6},{8,9},{9,8},{10,11... | collective-permute-start | bytes 405512 | tf_op jit(solution)/shard_map/ppermute | solution.py:25
  26.6 1.7 %collective-permute-start.6 = (bf16[264,256]{1,0:T(8,128)(2,1)S(1)}, bf16[264,256]{1,0:T(8,128)(2,1)S(1)}, u32[]{:S(2)}, u32[]{:S(2)}) collective-permute-start(bf16[264,256]{1,0:T(8,128)(2,1)S(1)} %collective-permute-done.5.refs_2_), channel_id=1, source_target_pairs={{0,1},{1,0},{2,3},{3,2},{4,5},{5,4},{6,7},{7,6},{8,9},{9,8},{10,11... | collective-permute-start | bytes 405512 | tf_op jit(solution)/shard_map/ppermute | solution.py:25

commit v3 on v2

--- a/solution.py
+++ b/solution.py
@@ -88,64 +88,90 @@
     return jnp.where(across == 0, 1.0, jnp.where(across == 1, in_first, 0.0)).astype(jnp.bfloat16)
 
 
-def attend_kernel(scale, heads, begin, end, n_pieces, q_ref, own_ref, *refs):
+def first_kernel(scale, heads, q_ref, own_ref, *refs):
+    *piece_refs, q_out, top_out, acc_out, keys_ref, values_ref = refs
     rows, width = own_ref.shape[1], own_ref.shape[1] // 2
+    ids = ids_of(own_ref)
+    first = ids[:, 0:1]
+    causal = causal_mask(own_ref)
+    own_keys, own_values = own_ref[0:rows, 0:width], wide_values(own_ref)
+    extra = query_extra(ids, first, rows, width)
+    for at, ref in enumerate(piece_refs):
+        here = slice(at * rows, (at + 1) * rows)
+        keys_ref[here, :] = wide_keys(ref, first, on_core_one() if at == 0 else 1.0)
+        values_ref[here, :] = wide_values(ref)
+    for head in range(heads):
+        here = slice(head * rows, (head + 1) * rows)
+        q = q_ref[:, head * width : (head + 1) * width]
+        wide = jnp.concatenate([q, extra], axis=1)
+        q_out[here, :] = wide
+        own_scores = jnp.where(causal, nt(q, own_keys), outside)
+        scores = nt(wide, keys_ref[...])
+        top = jnp.maximum(jnp.max(own_scores, axis=1, keepdims=True), jnp.max(scores, axis=1, keepdims=True))
+        acc = nn(jnp.exp2((own_scores - top) * scale).astype(jnp.bfloat16), own_values)
+        acc = acc + nn(jnp.exp2((scores - top) * scale).astype(jnp.bfloat16), values_ref[...])
+        top_out[here, :] = jnp.broadcast_to(top, (rows, width))
+        acc_out[here, :] = acc
+
+
+def next_kernel(scale, heads, end, sizes, q_ref, own_ref, *refs):
+    n_pieces = sum(sizes)
     piece_refs, refs = refs[:n_pieces], refs[n_pieces:]
-    if begin:
-        q_out, top_out, acc_out, keys_ref, values_ref = refs
-    elif end:
+    if end:
         top_in, acc_in, out_ref, keys_ref, values_ref, done_ref, sems = refs
     else:
         top_in, acc_in, top_out, acc_out, keys_ref, values_ref = refs
-    ids = ids_of(own_ref)
-    first = ids[:, 0:1]
-    if begin:
-        causal = causal_mask(own_ref)
-        own_keys, own_values = own_ref[0:rows, 0:width], wide_values(own_ref)
-        extra = query_extra(ids, first, rows, width)
-    for at, ref in enumerate(piece_refs):
-        here = slice(at * rows, (at + 1) * rows)
-        keys_ref[here, :] = wide_keys(ref, first, on_core_one() if begin and at == 0 else 1.0)
-        values_ref[here, :] = wide_values(ref)
-    copies = []
-    for head in range(heads):
-        here = slice(head * rows, (head + 1) * rows)
-        place = slice(head * width, (head + 1) * width)
-        if begin:
-            q = q_ref[:, place]
-            wide = jnp.concatenate([q, extra], axis=1)
-            q_out[here, :] = wide
-            own_scores = jnp.where(causal, nt(q, own_keys), outside)
-            before = jnp.max(own_scores, axis=1, keepdims=True)
-        else:
-            wide = q_ref[here, :]
-            before = top_in[here, 0:1]
-        scores = nt(wide, keys_ref[...])
-        top = jnp.maximum(before, jnp.max(scores, axis=1, keepdims=True))
-        acc = nn(jnp.exp2((scores - top) * scale).astype(jnp.bfloat16), values_ref[...])
-        if begin:
-            acc = acc + nn(jnp.exp2((own_scores - top) * scale).astype(jnp.bfloat16), own_values)
-        else:
-            acc = acc + acc_in[here, :] * jnp.exp2((before - top) * scale)
-        if end:
-            done_ref[:, place] = (acc[:, 0:width] / acc[:, width:]).astype(jnp.bfloat16)
-            copy = pltpu.make_async_copy(done_ref.at[:, place], out_ref.at[:, place], sems.at[head])
-            copy.start()
-            copies.append(copy)
-        else:
-            top_out[here, :] = jnp.broadcast_to(top, (rows, width))
-            acc_out[here, :] = acc
-    for copy in copies:
-        copy.wait()
-
-
-def call(scale, heads, begin, end, q, own, pieces, state):
+    rows, width = own_ref.shape[1], own_ref.shape[1] // 2
+    first = ids_of(own_ref)[:, 0:1]
+    level, at = jnp.zeros((1, 1), jnp.int32), 0
+    for step, size in enumerate(sizes):
+        matches = sum(count(ids_of(ref), first) for ref in piece_refs[at : at + size])
+        level = jnp.where(matches > 0.0, step + 1, level)
+        at += size
+    level = level[0, 0]
+
+    def go(n):
+        for at, ref in enumerate(piece_refs[:n]):
+            here = slice(at * rows, (at + 1) * rows)
+            keys_ref[here, :] = wide_keys(ref, first, 1.0)
+            values_ref[here, :] = wide_values(ref)
+        copies = []
+        for head in range(heads):
+            here = slice(head * rows, (head + 1) * rows)
+            place = slice(head * width, (head + 1) * width)
+            acc = acc_in[here, :]
+            if n:
+                before = top_in[here, 0:1]
+                scores = nt(q_ref[here, :], keys_ref[0 : n * rows, :])
+                top = jnp.maximum(before, jnp.max(scores, axis=1, keepdims=True))
+                acc = acc * jnp.exp2((before - top) * scale)
+                acc = acc + nn(jnp.exp2((scores - top) * scale).astype(jnp.bfloat16), values_ref[0 : n * rows, :])
+            if end:
+                done_ref[:, place] = (acc[:, 0:width] / acc[:, width:]).astype(jnp.bfloat16)
+                copy = pltpu.make_async_copy(done_ref.at[:, place], out_ref.at[:, place], sems.at[head])
+                copy.start()
+                copies.append(copy)
+            else:
+                top_out[here, :] = jnp.broadcast_to(top, (rows, width))
+                acc_out[here, :] = acc
+        for copy in copies:
+            copy.wait()
+
+    if not end:
+        return go(n_pieces)
+    for step in range(len(sizes) + 1):
+        pl.when(level == step)(functools.partial(go, sum(sizes[:step])))
+
+
+def call(scale, heads, begin, end, q, own, sizes, pieces, state):
     vmem = pl.BlockSpec(memory_space=pltpu.VMEM)
     rows, width = own.shape[1], own.shape[1] // 2
     shape, f32, bf16 = jax.ShapeDtypeStruct, jnp.float32, jnp.bfloat16
     outs = [shape((heads * rows, width), f32), shape((heads * rows, 2 * width), f32)]
+    kernel = functools.partial(next_kernel, scale, heads, end, sizes)
     if begin:
         outs.insert(0, shape((heads * rows, 2 * width), bf16))
+        kernel = functools.partial(first_kernel, scale, heads)
     scratch = [pltpu.VMEM((len(pieces) * rows, 2 * width), bf16)] * 2
     out_specs = [vmem] * len(outs)
     if end:
@@ -155,7 +181,7 @@
     moved = sum(math.prod(a.shape) * a.dtype.itemsize for a in (*args, *outs))
     flops = 8 * (len(pieces) + begin) * heads * rows * rows * width
     return pl.pallas_call(
-        functools.partial(attend_kernel, scale, heads, begin, end, len(pieces)),
+        kernel,
         out_shape=outs,
         in_specs=[vmem] * len(args),
         out_specs=out_specs,
@@ -171,7 +197,7 @@
     kv0 = pack(keys, values, doc_ids)
     kv4 = chips_on(kv0, 4, True)
     kv2 = chips_on(kv0, 2, False)
-    kv1 = chips_on(kv0, 1, False)
+    kv1 = chips_on(kv0, 1, True)
     kv3 = chips_on(kv4, -1, True)
     attend = functools.partial(call, scale, heads)
 
@@ -179,10 +205,10 @@
         return [piece, other_core(piece)]
 
     kv4t = other_core(kv4)
-    q, *state = attend(True, False, queries, kv0, [other_core(kv0), kv4], [])
+    q, *state = attend(True, False, queries, kv0, (2,), [other_core(kv0), kv4], [])
     q, state, kv1 = lax.optimization_barrier((q, state, kv1))
-    state = attend(False, False, q, kv0, [*both(kv1), kv4t], state)
-    (out,) = attend(False, True, q, kv0, [*both(kv2), *both(kv3)], state)
+    state = attend(False, False, q, kv0, (2, 1), [*both(kv1), kv4t], state)
+    (out,) = attend(False, True, q, kv0, (2, 2), [*both(kv2), *both(kv3)], state)
     return out
 
 

time: 31.3 us -> 30.7 us (0.981); the launches traced: 31.1 us -> 30.8 us
  starting transfers between devices: 15.3 us -> 13.9 us
  waiting for transfers between devices: 8.76 us -> 9.77 us
    ppermute x4, starting transfers between devices: 12.6 us -> 10.2 us  [chips_on(): lax.ppermute(value, axes, [(a, b) for a, b in pairs if wrap or b == a + s...]
    ppermute x5, starting transfers between devices: 2.66 us -> 3.69 us  [other_core(): return lax.ppermute(value, axes, [(d, d ^ 1) for d in range(count)])]
    ppermute x4, waiting for transfers between devices: 8.75 us -> 9.75 us  [chips_on(): lax.ppermute(value, axes, [(a, b) for a, b in pairs if wrap or b == a + s...]
  transfers between devices with their start and end apart: 9 -> 9, of which waited for: 2 -> 3; matrix products, arithmetic and copies ran while one was open for 0% -> 0% of each run, Pallas kernels for 10% -> 10%
where the time goes in v3:
time: 30.7 us; the launch traced here: 30.8 us
  starting transfers between devices  13.9 us (45%)
  waiting for transfers between devices  9.77 us (32%)
  Pallas kernels  6.2 us (20%)
  other arithmetic  0.94 us (3%)
    ppermute x4, starting transfers between devices, chips_on(): lax.ppermute(value, axes, [(a, b) for a, b in pairs if wrap or b == a + s...  10.2 us
    ppermute x4, waiting for transfers between devices, chips_on(): lax.ppermute(value, axes, [(a, b) for a, b in pairs if wrap or b == a + s...  9.75 us
    pallas_call x3, Pallas kernels, call(): pl.pallas_call(kernel, out_shape=outs, in_specs=[vmem] * len(args), out_s...  6.2 us
    ppermute x5, starting transfers between devices, other_core(): return lax.ppermute(value, axes, [(d, d ^ 1) for d in range(count)])  3.69 us
    concatenate x1, other arithmetic, pack(): jnp.concatenate([keys, values], axis=1)  0.93 us
  transfers between devices with their start and end apart: 9, of which 3 were waited for; matrix products, arithmetic and copies ran while one was open for 0% of the time, Pallas kernels for 10%

profile of v3, /device:TPU:35, one launch (start us, length us, event | category | flops | bytes accessed | tf_op | source)
XLA Modules:
  0.0 30.8 jit_solution(9764016432440694129)
XLA Ops:
  0.0 0.9 %fusion.2 = bf16[264,256]{1,0:T(8,128)(2,1)S(1)} fusion(bf16[256,128]{1,0:T(8,128)(2,1)} %param.6, bf16[256,128]{1,0:T(8,128)(2,1)} %param.5), kind=kLoop, calls=%fused_computation.3 | loop fusion | flops 473088 | bytes 266240 | tf_op jit(solution)/shard_map/concatenate | solution.py:30
  0.9 0.0 copy-done.1
  1.0 6.1 %collective-permute-start.1 = (bf16[264,256]{1,0:T(8,128)(2,1)S(1)}, bf16[264,256]{1,0:T(8,128)(2,1)S(1)}, u32[]{:S(2)}, u32[]{:S(2)}) collective-permute-start(bf16[264,256]{1,0:T(8,128)(2,1)S(1)} %broadcast_dynamic-update-slice_fusion.own_ref), channel_id=1, source_target_pairs={{0,8},{1,9},{2,10},{3,11},{4,12},{5,13},{6,14},{7,15},{8,16},{9,17... | collective-permute-start | bytes 405512 | tf_op jit(solution)/shard_map/ppermute | solution.py:20
  7.1 1.0 %collective-permute-start = (bf16[264,256]{1,0:T(8,128)(2,1)S(1)}, bf16[264,256]{1,0:T(8,128)(2,1)S(1)}, u32[]{:S(2)}, u32[]{:S(2)}) collective-permute-start(bf16[264,256]{1,0:T(8,128)(2,1)S(1)} %broadcast_dynamic-update-slice_fusion.own_ref), channel_id=1, source_target_pairs={{0,1},{1,0},{2,3},{3,2},{4,5},{5,4},{6,7},{7,6},{8,9},{9,8},{10,11... | collective-permute-start | bytes 405512 | tf_op jit(solution)/shard_map/ppermute | solution.py:25
  8.0 0.7 %collective-permute-start.2 = (bf16[264,256]{1,0:T(8,128)(2,1)S(1)}, bf16[264,256]{1,0:T(8,128)(2,1)S(1)}, u32[]{:S(2)}, u32[]{:S(2)}) collective-permute-start(bf16[264,256]{1,0:T(8,128)(2,1)S(1)} %broadcast_dynamic-update-slice_fusion.own_ref), channel_id=1, source_target_pairs={{0,2},{1,3},{2,4},{3,5},{4,6},{5,7},{6,8},{7,9},{8,10},{9,11},{10,... | collective-permute-start | bytes 405512 | tf_op jit(solution)/shard_map/ppermute | solution.py:20
  8.8 2.4 %collective-permute-start.3 = (bf16[264,256]{1,0:T(8,128)(2,1)S(1)}, bf16[264,256]{1,0:T(8,128)(2,1)S(1)}, u32[]{:S(2)}, u32[]{:S(2)}) collective-permute-start(bf16[264,256]{1,0:T(8,128)(2,1)S(1)} %broadcast_dynamic-update-slice_fusion.own_ref), channel_id=1, source_target_pairs={{0,4},{1,5},{2,6},{3,7},{4,8},{5,9},{6,10},{7,11},{8,12},{9,13},{1... | collective-permute-start | bytes 405512 | tf_op jit(solution)/shard_map/ppermute | solution.py:20
  11.1 1.4 %collective-permute-done.1.refs_1_ = bf16[264,256]{1,0:T(8,128)(2,1)S(1)} collective-permute-done((bf16[264,256]{1,0:T(8,128)(2,1)S(1)}, bf16[264,256]{1,0:T(8,128)(2,1)S(1)}, u32[]{:S(2)}, u32[]{:S(2)}) %collective-permute-start.1) | collective-permute-done | bytes 135200 | tf_op jit(solution)/shard_map/ppermute | solution.py:20
  12.5 1.0 %collective-permute-start.5 = (bf16[264,256]{1,0:T(8,128)(2,1)S(1)}, bf16[264,256]{1,0:T(8,128)(2,1)S(1)}, u32[]{:S(2)}, u32[]{:S(2)}) collective-permute-start(bf16[264,256]{1,0:T(8,128)(2,1)S(1)} %collective-permute-done.1.refs_1_), channel_id=1, source_target_pairs={{0,254},{1,255},{2,0},{3,1},{4,2},{5,3},{6,4},{7,5},{8,6},{9,7},{1... | collective-permute-start | bytes 405512 | tf_op jit(solution)/shard_map/ppermute | solution.py:20
  13.5 0.0 collective-permute-done.refs_0_
  13.5 0.0 copy-done
  13.5 1.5 %shard_map.46 = (bf16[1024,256]{1,0:T(8,128)(2,1)S(1)}, f32[1024,128]{1,0:T(8,128)S(1)}, f32[1024,256]{1,0:T(8,128)S(1)}) custom-call(bf16[256,512]{1,0:T(8,128)(2,1)S(1)} %copy-done, bf16[264,256]{1,0:T(8,128)(2,1)S(1)} %broadcast_dynamic-update-slice_fusion.own_ref, bf16[264,256]{1,0:T(8,128)(2,1)S(1)} %collective-permute-done.refs_0_, ...), custom_call_target="tpu_custom_call" | custom-call | flops 805306368 | bytes 2764800 | tf_op jit(solution)/shard_map/pallas_call | solution.py:183
  15.1 2.0 %collective-permute-done.2.refs_0_ = bf16[264,256]{1,0:T(8,128)(2,1)S(1)} collective-permute-done((bf16[264,256]{1,0:T(8,128)(2,1)S(1)}, bf16[264,256]{1,0:T(8,128)(2,1)S(1)}, u32[]{:S(2)}, u32[]{:S(2)}) %collective-permute-start.2) | collective-permute-done | bytes 135200 | tf_op jit(solution)/shard_map/ppermute | solution.py:20
  17.1 2.2 %collective-permute-start.7 = (bf16[264,256]{1,0:T(8,128)(2,1)S(1)}, bf16[264,256]{1,0:T(8,128)(2,1)S(1)}, u32[]{:S(2)}, u32[]{:S(2)}) collective-permute-start(bf16[264,256]{1,0:T(8,128)(2,1)S(1)} %collective-permute-done.2.refs_0_), channel_id=1, source_target_pairs={{0,1},{1,0},{2,3},{3,2},{4,5},{5,4},{6,7},{7,6},{8,9},{9,8},{10,11... | collective-permute-start | bytes 405512 | tf_op jit(solution)/shard_map/ppermute | solution.py:25
  19.3 0.0 collective-permute-start.8
  19.3 6.3 %collective-permute-done.3.refs_0_ = bf16[264,256]{1,0:T(8,128)(2,1)S(1)} collective-permute-done((bf16[264,256]{1,0:T(8,128)(2,1)S(1)}, bf16[264,256]{1,0:T(8,128)(2,1)S(1)}, u32[]{:S(2)}, u32[]{:S(2)}) %collective-permute-start.3) | collective-permute-done | bytes 135200 | tf_op jit(solution)/shard_map/ppermute | solution.py:20
  25.6 0.5 %collective-permute-start.4 = (bf16[264,256]{1,0:T(8,128)(2,1)S(1)}, bf16[264,256]{1,0:T(8,128)(2,1)S(1)}, u32[]{:S(2)}, u32[]{:S(2)}) collective-permute-start(bf16[264,256]{1,0:T(8,128)(2,1)S(1)} %collective-permute-done.3.refs_0_), channel_id=1, source_target_pairs={{0,1},{1,0},{2,3},{3,2},{4,5},{5,4},{6,7},{7,6},{8,9},{9,8},{10,11... | collective-permute-start | bytes 405512 | tf_op jit(solution)/shard_map/ppermute | solution.py:25
  26.1 0.0 collective-permute-done.5.refs_2_
  26.1 0.0 collective-permute-start.6
  26.1 0.0 collective-permute-done.7.refs_1_
  26.1 0.0 collective-permute-done.8.refs_2_
  26.1 1.7 %shard_map.47 = (f32[1024,128]{1,0:T(8,128)S(1)}, f32[1024,256]{1,0:T(8,128)S(1)}) custom-call(bf16[1024,256]{1,0:T(8,128)(2,1)S(1)} %get-tuple-element.21.q_ref, bf16[264,256]{1,0:T(8,128)(2,1)S(1)} %broadcast_dynamic-update-slice_fusion.own_ref, bf16[264,256]{1,0:T(8,128)(2,1)S(1)} %collective-permute-done.2.refs_0_, ...), custom_call_target="tpu_custom_call" | custom-call | flops 805306368 | bytes 4210688 | tf_op jit(solution)/shard_map/pallas_call | solution.py:183
  27.8 0.0 collective-permute-done.4.refs_1_
  27.9 0.0 collective-permute-done.6.refs_3_
  27.9 3.0 %shard_map.48 = bf16[256,512]{1,0:T(8,128)(2,1)} custom-call(bf16[1024,256]{1,0:T(8,128)(2,1)S(1)} %get-tuple-element.21.q_ref, bf16[264,256]{1,0:T(8,128)(2,1)S(1)} %broadcast_dynamic-update-slice_fusion.own_ref, bf16[264,256]{1,0:T(8,128)(2,1)S(1)} %collective-permute-done.3.refs_0_, bf16[264,256]{1,0:T(8,128)(2,1)S(1)} %collective-permute-done.4.refs_1_, ...), custom_call_target="tpu_custom_call" | custom-call | flops 1073741824 | bytes 3035136 | tf_op jit(solution)/shard_map/pallas_call | solution.py:183
  (4 shorter events, 0.0 us)
Async XLA Ops:
  0.0 0.9 %copy-start.1 = (s32[256]{0:T(256)S(1)}, s32[256]{0:T(256)}, u32[]{:S(2)}) copy-start(s32[256]{0:T(256)} %param.7) | copy-start | bytes 3076
  0.0 13.5 %copy-start = (bf16[256,512]{1,0:T(8,128)(2,1)S(1)}, bf16[256,512]{1,0:T(8,128)(2,1)}, u32[]{:S(2)}) copy-start(bf16[256,512]{1,0:T(8,128)(2,1)} %q_ref.1) | copy-start | bytes 786436
  1.0 11.6 %collective-permute-start.1 = (bf16[264,256]{1,0:T(8,128)(2,1)S(1)}, bf16[264,256]{1,0:T(8,128)(2,1)S(1)}, u32[]{:S(2)}, u32[]{:S(2)}) collective-permute-start(bf16[264,256]{1,0:T(8,128)(2,1)S(1)} %broadcast_dynamic-update-slice_fusion.own_ref), channel_id=1, source_target_pairs={{0,8},{1,9},{2,10},{3,11},{4,12},{5,13},{6,14},{7,15},{8,16},{9,17... | collective-permute-start | bytes 405512 | tf_op jit(solution)/shard_map/ppermute | solution.py:20
  7.1 6.5 %collective-permute-start = (bf16[264,256]{1,0:T(8,128)(2,1)S(1)}, bf16[264,256]{1,0:T(8,128)(2,1)S(1)}, u32[]{:S(2)}, u32[]{:S(2)}) collective-permute-start(bf16[264,256]{1,0:T(8,128)(2,1)S(1)} %broadcast_dynamic-update-slice_fusion.own_ref), channel_id=1, source_target_pairs={{0,1},{1,0},{2,3},{3,2},{4,5},{5,4},{6,7},{7,6},{8,9},{9,8},{10,11... | collective-permute-start | bytes 405512 | tf_op jit(solution)/shard_map/ppermute | solution.py:25
  8.0 9.0 %collective-permute-start.2 = (bf16[264,256]{1,0:T(8,128)(2,1)S(1)}, bf16[264,256]{1,0:T(8,128)(2,1)S(1)}, u32[]{:S(2)}, u32[]{:S(2)}) collective-permute-start(bf16[264,256]{1,0:T(8,128)(2,1)S(1)} %broadcast_dynamic-update-slice_fusion.own_ref), channel_id=1, source_target_pairs={{0,2},{1,3},{2,4},{3,5},{4,6},{5,7},{6,8},{7,9},{8,10},{9,11},{10,... | collective-permute-start | bytes 405512 | tf_op jit(solution)/shard_map/ppermute | solution.py:20
  8.8 16.9 %collective-permute-start.3 = (bf16[264,256]{1,0:T(8,128)(2,1)S(1)}, bf16[264,256]{1,0:T(8,128)(2,1)S(1)}, u32[]{:S(2)}, u32[]{:S(2)}) collective-permute-start(bf16[264,256]{1,0:T(8,128)(2,1)S(1)} %broadcast_dynamic-update-slice_fusion.own_ref), channel_id=1, source_target_pairs={{0,4},{1,5},{2,6},{3,7},{4,8},{5,9},{6,10},{7,11},{8,12},{9,13},{1... | collective-permute-start | bytes 405512 | tf_op jit(solution)/shard_map/ppermute | solution.py:20
  12.5 13.6 %collective-permute-start.5 = (bf16[264,256]{1,0:T(8,128)(2,1)S(1)}, bf16[264,256]{1,0:T(8,128)(2,1)S(1)}, u32[]{:S(2)}, u32[]{:S(2)}) collective-permute-start(bf16[264,256]{1,0:T(8,128)(2,1)S(1)} %collective-permute-done.1.refs_1_), channel_id=1, source_target_pairs={{0,254},{1,255},{2,0},{3,1},{4,2},{5,3},{6,4},{7,5},{8,6},{9,7},{1... | collective-permute-start | bytes 405512 | tf_op jit(solution)/shard_map/ppermute | solution.py:20
  17.1 9.1 %collective-permute-start.7 = (bf16[264,256]{1,0:T(8,128)(2,1)S(1)}, bf16[264,256]{1,0:T(8,128)(2,1)S(1)}, u32[]{:S(2)}, u32[]{:S(2)}) collective-permute-start(bf16[264,256]{1,0:T(8,128)(2,1)S(1)} %collective-permute-done.2.refs_0_), channel_id=1, source_target_pairs={{0,1},{1,0},{2,3},{3,2},{4,5},{5,4},{6,7},{7,6},{8,9},{9,8},{10,11... | collective-permute-start | bytes 405512 | tf_op jit(solution)/shard_map/ppermute | solution.py:25
  19.3 6.9 %collective-permute-start.8 = (bf16[264,256]{1,0:T(8,128)(2,1)S(1)}, bf16[264,256]{1,0:T(8,128)(2,1)S(1)}, u32[]{:S(2)}, u32[]{:S(2)}) collective-permute-start(bf16[264,256]{1,0:T(8,128)(2,1)S(1)} %collective-permute-done.1.refs_1_), channel_id=1, source_target_pairs={{0,1},{1,0},{2,3},{3,2},{4,5},{5,4},{6,7},{7,6},{8,9},{9,8},{10,11... | collective-permute-start | bytes 405512 | tf_op jit(solution)/shard_map/ppermute | solution.py:25
  25.6 2.2 %collective-permute-start.4 = (bf16[264,256]{1,0:T(8,128)(2,1)S(1)}, bf16[264,256]{1,0:T(8,128)(2,1)S(1)}, u32[]{:S(2)}, u32[]{:S(2)}) collective-permute-start(bf16[264,256]{1,0:T(8,128)(2,1)S(1)} %collective-permute-done.3.refs_0_), channel_id=1, source_target_pairs={{0,1},{1,0},{2,3},{3,2},{4,5},{5,4},{6,7},{7,6},{8,9},{9,8},{10,11... | collective-permute-start | bytes 405512 | tf_op jit(solution)/shard_map/ppermute | solution.py:25
  26.1 1.7 %collective-permute-start.6 = (bf16[264,256]{1,0:T(8,128)(2,1)S(1)}, bf16[264,256]{1,0:T(8,128)(2,1)S(1)}, u32[]{:S(2)}, u32[]{:S(2)}) collective-permute-start(bf16[264,256]{1,0:T(8,128)(2,1)S(1)} %collective-permute-done.5.refs_2_), channel_id=1, source_target_pairs={{0,1},{1,0},{2,3},{3,2},{4,5},{5,4},{6,7},{7,6},{8,9},{9,8},{10,11... | collective-permute-start | bytes 405512 | tf_op jit(solution)/shard_map/ppermute | solution.py:25

commit v4 on v3

--- a/solution.py
+++ b/solution.py
@@ -136,13 +136,20 @@
             keys_ref[here, :] = wide_keys(ref, first, 1.0)
             values_ref[here, :] = wide_values(ref)
         copies = []
+
+        def scores_of(head):
+            return nt(q_ref[head * rows : (head + 1) * rows, :], keys_ref[0 : n * rows, :])
+
+        ahead = scores_of(0) if n else None
         for head in range(heads):
             here = slice(head * rows, (head + 1) * rows)
             place = slice(head * width, (head + 1) * width)
             acc = acc_in[here, :]
             if n:
+                scores = ahead
                 before = top_in[here, 0:1]
-                scores = nt(q_ref[here, :], keys_ref[0 : n * rows, :])
+                if head + 1 < heads:
+                    ahead = scores_of(head + 1)
                 top = jnp.maximum(before, jnp.max(scores, axis=1, keepdims=True))
                 acc = acc * jnp.exp2((before - top) * scale)
                 acc = acc + nn(jnp.exp2((scores - top) * scale).astype(jnp.bfloat16), values_ref[0 : n * rows, :])
@@ -151,7 +158,7 @@
                 copy = pltpu.make_async_copy(done_ref.at[:, place], out_ref.at[:, place], sems.at[head])
                 copy.start()
                 copies.append(copy)
-            else:
+            elif n:
                 top_out[here, :] = jnp.broadcast_to(top, (rows, width))
                 acc_out[here, :] = acc
         for copy in copies:

time: 30.7 us -> 30.5 us (level)
  no operation moved by 1% of the time
where the time goes in v4:
time: 30.5 us; the launch traced here: 30.6 us
  starting transfers between devices  13.9 us (46%)
  waiting for transfers between devices  9.77 us (32%)
  Pallas kernels  5.92 us (19%)
  other arithmetic  0.94 us (3%)
    ppermute x4, starting transfers between devices, chips_on(): lax.ppermute(value, axes, [(a, b) for a, b in pairs if wrap or b == a + s...  10.2 us
    ppermute x4, waiting for transfers between devices, chips_on(): lax.ppermute(value, axes, [(a, b) for a, b in pairs if wrap or b == a + s...  9.75 us
    pallas_call x3, Pallas kernels, call(): pl.pallas_call(kernel, out_shape=outs, in_specs=[vmem] * len(args), out_s...  5.92 us
    ppermute x5, starting transfers between devices, other_core(): return lax.ppermute(value, axes, [(d, d ^ 1) for d in range(count)])  3.69 us
    concatenate x1, other arithmetic, pack(): jnp.concatenate([keys, values], axis=1)  0.93 us
  transfers between devices with their start and end apart: 9, of which 3 were waited for; matrix products, arithmetic and copies ran while one was open for 0% of the time, Pallas kernels for 10%

profile of v4, /device:TPU:35, one launch (start us, length us, event | category | flops | bytes accessed | tf_op | source)
XLA Modules:
  0.0 30.6 jit_solution(12308234819710202221)
XLA Ops:
  0.0 0.9 %fusion.2 = bf16[264,256]{1,0:T(8,128)(2,1)S(1)} fusion(bf16[256,128]{1,0:T(8,128)(2,1)} %param.6, bf16[256,128]{1,0:T(8,128)(2,1)} %param.5), kind=kLoop, calls=%fused_computation.3 | loop fusion | flops 473088 | bytes 266240 | tf_op jit(solution)/shard_map/concatenate | solution.py:30
  0.9 0.0 copy-done.1
  1.0 6.1 %collective-permute-start.1 = (bf16[264,256]{1,0:T(8,128)(2,1)S(1)}, bf16[264,256]{1,0:T(8,128)(2,1)S(1)}, u32[]{:S(2)}, u32[]{:S(2)}) collective-permute-start(bf16[264,256]{1,0:T(8,128)(2,1)S(1)} %broadcast_dynamic-update-slice_fusion.own_ref), channel_id=1, source_target_pairs={{0,8},{1,9},{2,10},{3,11},{4,12},{5,13},{6,14},{7,15},{8,16},{9,17... | collective-permute-start | bytes 405512 | tf_op jit(solution)/shard_map/ppermute | solution.py:20
  7.1 1.0 %collective-permute-start = (bf16[264,256]{1,0:T(8,128)(2,1)S(1)}, bf16[264,256]{1,0:T(8,128)(2,1)S(1)}, u32[]{:S(2)}, u32[]{:S(2)}) collective-permute-start(bf16[264,256]{1,0:T(8,128)(2,1)S(1)} %broadcast_dynamic-update-slice_fusion.own_ref), channel_id=1, source_target_pairs={{0,1},{1,0},{2,3},{3,2},{4,5},{5,4},{6,7},{7,6},{8,9},{9,8},{10,11... | collective-permute-start | bytes 405512 | tf_op jit(solution)/shard_map/ppermute | solution.py:25
  8.0 0.7 %collective-permute-start.2 = (bf16[264,256]{1,0:T(8,128)(2,1)S(1)}, bf16[264,256]{1,0:T(8,128)(2,1)S(1)}, u32[]{:S(2)}, u32[]{:S(2)}) collective-permute-start(bf16[264,256]{1,0:T(8,128)(2,1)S(1)} %broadcast_dynamic-update-slice_fusion.own_ref), channel_id=1, source_target_pairs={{0,2},{1,3},{2,4},{3,5},{4,6},{5,7},{6,8},{7,9},{8,10},{9,11},{10,... | collective-permute-start | bytes 405512 | tf_op jit(solution)/shard_map/ppermute | solution.py:20
  8.8 2.4 %collective-permute-start.3 = (bf16[264,256]{1,0:T(8,128)(2,1)S(1)}, bf16[264,256]{1,0:T(8,128)(2,1)S(1)}, u32[]{:S(2)}, u32[]{:S(2)}) collective-permute-start(bf16[264,256]{1,0:T(8,128)(2,1)S(1)} %broadcast_dynamic-update-slice_fusion.own_ref), channel_id=1, source_target_pairs={{0,4},{1,5},{2,6},{3,7},{4,8},{5,9},{6,10},{7,11},{8,12},{9,13},{1... | collective-permute-start | bytes 405512 | tf_op jit(solution)/shard_map/ppermute | solution.py:20
  11.1 1.4 %collective-permute-done.1.refs_1_ = bf16[264,256]{1,0:T(8,128)(2,1)S(1)} collective-permute-done((bf16[264,256]{1,0:T(8,128)(2,1)S(1)}, bf16[264,256]{1,0:T(8,128)(2,1)S(1)}, u32[]{:S(2)}, u32[]{:S(2)}) %collective-permute-start.1) | collective-permute-done | bytes 135200 | tf_op jit(solution)/shard_map/ppermute | solution.py:20
  12.5 1.0 %collective-permute-start.5 = (bf16[264,256]{1,0:T(8,128)(2,1)S(1)}, bf16[264,256]{1,0:T(8,128)(2,1)S(1)}, u32[]{:S(2)}, u32[]{:S(2)}) collective-permute-start(bf16[264,256]{1,0:T(8,128)(2,1)S(1)} %collective-permute-done.1.refs_1_), channel_id=1, source_target_pairs={{0,254},{1,255},{2,0},{3,1},{4,2},{5,3},{6,4},{7,5},{8,6},{9,7},{1... | collective-permute-start | bytes 405512 | tf_op jit(solution)/shard_map/ppermute | solution.py:20
  13.5 0.0 collective-permute-done.refs_0_
  13.5 0.0 copy-done
  13.5 1.5 %shard_map.46 = (bf16[1024,256]{1,0:T(8,128)(2,1)S(1)}, f32[1024,128]{1,0:T(8,128)S(1)}, f32[1024,256]{1,0:T(8,128)S(1)}) custom-call(bf16[256,512]{1,0:T(8,128)(2,1)S(1)} %copy-done, bf16[264,256]{1,0:T(8,128)(2,1)S(1)} %broadcast_dynamic-update-slice_fusion.own_ref, bf16[264,256]{1,0:T(8,128)(2,1)S(1)} %collective-permute-done.refs_0_, ...), custom_call_target="tpu_custom_call" | custom-call | flops 805306368 | bytes 2764800 | tf_op jit(solution)/shard_map/pallas_call | solution.py:190
  15.1 2.0 %collective-permute-done.2.refs_0_ = bf16[264,256]{1,0:T(8,128)(2,1)S(1)} collective-permute-done((bf16[264,256]{1,0:T(8,128)(2,1)S(1)}, bf16[264,256]{1,0:T(8,128)(2,1)S(1)}, u32[]{:S(2)}, u32[]{:S(2)}) %collective-permute-start.2) | collective-permute-done | bytes 135200 | tf_op jit(solution)/shard_map/ppermute | solution.py:20
  17.1 2.2 %collective-permute-start.7 = (bf16[264,256]{1,0:T(8,128)(2,1)S(1)}, bf16[264,256]{1,0:T(8,128)(2,1)S(1)}, u32[]{:S(2)}, u32[]{:S(2)}) collective-permute-start(bf16[264,256]{1,0:T(8,128)(2,1)S(1)} %collective-permute-done.2.refs_0_), channel_id=1, source_target_pairs={{0,1},{1,0},{2,3},{3,2},{4,5},{5,4},{6,7},{7,6},{8,9},{9,8},{10,11... | collective-permute-start | bytes 405512 | tf_op jit(solution)/shard_map/ppermute | solution.py:25
  19.3 0.0 collective-permute-start.8
  19.3 6.3 %collective-permute-done.3.refs_0_ = bf16[264,256]{1,0:T(8,128)(2,1)S(1)} collective-permute-done((bf16[264,256]{1,0:T(8,128)(2,1)S(1)}, bf16[264,256]{1,0:T(8,128)(2,1)S(1)}, u32[]{:S(2)}, u32[]{:S(2)}) %collective-permute-start.3) | collective-permute-done | bytes 135200 | tf_op jit(solution)/shard_map/ppermute | solution.py:20
  25.6 0.5 %collective-permute-start.4 = (bf16[264,256]{1,0:T(8,128)(2,1)S(1)}, bf16[264,256]{1,0:T(8,128)(2,1)S(1)}, u32[]{:S(2)}, u32[]{:S(2)}) collective-permute-start(bf16[264,256]{1,0:T(8,128)(2,1)S(1)} %collective-permute-done.3.refs_0_), channel_id=1, source_target_pairs={{0,1},{1,0},{2,3},{3,2},{4,5},{5,4},{6,7},{7,6},{8,9},{9,8},{10,11... | collective-permute-start | bytes 405512 | tf_op jit(solution)/shard_map/ppermute | solution.py:25
  26.1 0.0 collective-permute-done.5.refs_2_
  26.1 0.0 collective-permute-start.6
  26.1 0.0 collective-permute-done.7.refs_1_
  26.1 0.0 collective-permute-done.8.refs_2_
  26.1 1.5 %shard_map.47 = (f32[1024,128]{1,0:T(8,128)S(1)}, f32[1024,256]{1,0:T(8,128)S(1)}) custom-call(bf16[1024,256]{1,0:T(8,128)(2,1)S(1)} %get-tuple-element.21.q_ref, bf16[264,256]{1,0:T(8,128)(2,1)S(1)} %broadcast_dynamic-update-slice_fusion.own_ref, bf16[264,256]{1,0:T(8,128)(2,1)S(1)} %collective-permute-done.2.refs_0_, ...), custom_call_target="tpu_custom_call" | custom-call | flops 805306368 | bytes 4210688 | tf_op jit(solution)/shard_map/pallas_call | solution.py:190
  27.7 0.0 collective-permute-done.4.refs_1_
  27.7 0.0 collective-permute-done.6.refs_3_
  27.7 2.9 %shard_map.48 = bf16[256,512]{1,0:T(8,128)(2,1)} custom-call(bf16[1024,256]{1,0:T(8,128)(2,1)S(1)} %get-tuple-element.21.q_ref, bf16[264,256]{1,0:T(8,128)(2,1)S(1)} %broadcast_dynamic-update-slice_fusion.own_ref, bf16[264,256]{1,0:T(8,128)(2,1)S(1)} %collective-permute-done.3.refs_0_, bf16[264,256]{1,0:T(8,128)(2,1)S(1)} %collective-permute-done.4.refs_1_, ...), custom_call_target="tpu_custom_call" | custom-call | flops 1073741824 | bytes 3035136 | tf_op jit(solution)/shard_map/pallas_call | solution.py:190
  (4 shorter events, 0.0 us)
Async XLA Ops:
  0.0 0.9 %copy-start.1 = (s32[256]{0:T(256)S(1)}, s32[256]{0:T(256)}, u32[]{:S(2)}) copy-start(s32[256]{0:T(256)} %param.7) | copy-start | bytes 3076
  0.0 13.5 %copy-start = (bf16[256,512]{1,0:T(8,128)(2,1)S(1)}, bf16[256,512]{1,0:T(8,128)(2,1)}, u32[]{:S(2)}) copy-start(bf16[256,512]{1,0:T(8,128)(2,1)} %q_ref.1) | copy-start | bytes 786436
  1.0 11.6 %collective-permute-start.1 = (bf16[264,256]{1,0:T(8,128)(2,1)S(1)}, bf16[264,256]{1,0:T(8,128)(2,1)S(1)}, u32[]{:S(2)}, u32[]{:S(2)}) collective-permute-start(bf16[264,256]{1,0:T(8,128)(2,1)S(1)} %broadcast_dynamic-update-slice_fusion.own_ref), channel_id=1, source_target_pairs={{0,8},{1,9},{2,10},{3,11},{4,12},{5,13},{6,14},{7,15},{8,16},{9,17... | collective-permute-start | bytes 405512 | tf_op jit(solution)/shard_map/ppermute | solution.py:20
  7.1 6.5 %collective-permute-start = (bf16[264,256]{1,0:T(8,128)(2,1)S(1)}, bf16[264,256]{1,0:T(8,128)(2,1)S(1)}, u32[]{:S(2)}, u32[]{:S(2)}) collective-permute-start(bf16[264,256]{1,0:T(8,128)(2,1)S(1)} %broadcast_dynamic-update-slice_fusion.own_ref), channel_id=1, source_target_pairs={{0,1},{1,0},{2,3},{3,2},{4,5},{5,4},{6,7},{7,6},{8,9},{9,8},{10,11... | collective-permute-start | bytes 405512 | tf_op jit(solution)/shard_map/ppermute | solution.py:25
  8.0 9.0 %collective-permute-start.2 = (bf16[264,256]{1,0:T(8,128)(2,1)S(1)}, bf16[264,256]{1,0:T(8,128)(2,1)S(1)}, u32[]{:S(2)}, u32[]{:S(2)}) collective-permute-start(bf16[264,256]{1,0:T(8,128)(2,1)S(1)} %broadcast_dynamic-update-slice_fusion.own_ref), channel_id=1, source_target_pairs={{0,2},{1,3},{2,4},{3,5},{4,6},{5,7},{6,8},{7,9},{8,10},{9,11},{10,... | collective-permute-start | bytes 405512 | tf_op jit(solution)/shard_map/ppermute | solution.py:20
  8.8 16.9 %collective-permute-start.3 = (bf16[264,256]{1,0:T(8,128)(2,1)S(1)}, bf16[264,256]{1,0:T(8,128)(2,1)S(1)}, u32[]{:S(2)}, u32[]{:S(2)}) collective-permute-start(bf16[264,256]{1,0:T(8,128)(2,1)S(1)} %broadcast_dynamic-update-slice_fusion.own_ref), channel_id=1, source_target_pairs={{0,4},{1,5},{2,6},{3,7},{4,8},{5,9},{6,10},{7,11},{8,12},{9,13},{1... | collective-permute-start | bytes 405512 | tf_op jit(solution)/shard_map/ppermute | solution.py:20
  12.5 13.6 %collective-permute-start.5 = (bf16[264,256]{1,0:T(8,128)(2,1)S(1)}, bf16[264,256]{1,0:T(8,128)(2,1)S(1)}, u32[]{:S(2)}, u32[]{:S(2)}) collective-permute-start(bf16[264,256]{1,0:T(8,128)(2,1)S(1)} %collective-permute-done.1.refs_1_), channel_id=1, source_target_pairs={{0,254},{1,255},{2,0},{3,1},{4,2},{5,3},{6,4},{7,5},{8,6},{9,7},{1... | collective-permute-start | bytes 405512 | tf_op jit(solution)/shard_map/ppermute | solution.py:20
  17.1 9.1 %collective-permute-start.7 = (bf16[264,256]{1,0:T(8,128)(2,1)S(1)}, bf16[264,256]{1,0:T(8,128)(2,1)S(1)}, u32[]{:S(2)}, u32[]{:S(2)}) collective-permute-start(bf16[264,256]{1,0:T(8,128)(2,1)S(1)} %collective-permute-done.2.refs_0_), channel_id=1, source_target_pairs={{0,1},{1,0},{2,3},{3,2},{4,5},{5,4},{6,7},{7,6},{8,9},{9,8},{10,11... | collective-permute-start | bytes 405512 | tf_op jit(solution)/shard_map/ppermute | solution.py:25
  19.3 6.9 %collective-permute-start.8 = (bf16[264,256]{1,0:T(8,128)(2,1)S(1)}, bf16[264,256]{1,0:T(8,128)(2,1)S(1)}, u32[]{:S(2)}, u32[]{:S(2)}) collective-permute-start(bf16[264,256]{1,0:T(8,128)(2,1)S(1)} %collective-permute-done.1.refs_1_), channel_id=1, source_target_pairs={{0,1},{1,0},{2,3},{3,2},{4,5},{5,4},{6,7},{7,6},{8,9},{9,8},{10,11... | collective-permute-start | bytes 405512 | tf_op jit(solution)/shard_map/ppermute | solution.py:25
  25.6 2.1 %collective-permute-start.4 = (bf16[264,256]{1,0:T(8,128)(2,1)S(1)}, bf16[264,256]{1,0:T(8,128)(2,1)S(1)}, u32[]{:S(2)}, u32[]{:S(2)}) collective-permute-start(bf16[264,256]{1,0:T(8,128)(2,1)S(1)} %collective-permute-done.3.refs_0_), channel_id=1, source_target_pairs={{0,1},{1,0},{2,3},{3,2},{4,5},{5,4},{6,7},{7,6},{8,9},{9,8},{10,11... | collective-permute-start | bytes 405512 | tf_op jit(solution)/shard_map/ppermute | solution.py:25
  26.1 1.6 %collective-permute-start.6 = (bf16[264,256]{1,0:T(8,128)(2,1)S(1)}, bf16[264,256]{1,0:T(8,128)(2,1)S(1)}, u32[]{:S(2)}, u32[]{:S(2)}) collective-permute-start(bf16[264,256]{1,0:T(8,128)(2,1)S(1)} %collective-permute-done.5.refs_2_), channel_id=1, source_target_pairs={{0,1},{1,0},{2,3},{3,2},{4,5},{5,4},{6,7},{7,6},{8,9},{9,8},{10,11... | collective-permute-start | bytes 405512 | tf_op jit(solution)/shard_map/ppermute | solution.py:25
